TPU v7x, 256 devices: a whole 4x4x8 slice. The times are simulated.
256 devices in a mesh: ctx: 128 (over x, y_lo, z, core), head: 2 (over y_hi).
Axes of the slice: x: 4, y: 4 (y_hi: 2, y_lo: 2; y = y_hi * 2 + y_lo), z: 8, core: 2. Of those that a mesh axis runs over, the one named last changes fastest.
Arguments:
- queries: bfloat16 [16384, 2048], P('ctx', 'head'), may hold values from -5 to 5
- key_vectors: bfloat16 [16384, 2048], P('ctx', 'head'), may hold values from -5 to 5
- value_vectors: bfloat16 [16384, 2048], P('ctx', 'head'), may hold values from -12 to 12
- slopes: float32 [16], P('head'), may hold values from 0.15 to 1.5
- w_out: bfloat16 [2048, 2048], P('head'), may hold values from -0.125 to 0.125
- grad_out: bfloat16 [16384, 2048], P('ctx', 'head'), may hold values from -6 to 6
Outputs:
- layer_out: bfloat16 [16384, 2048], P('ctx', 'head')
- grad_queries: bfloat16 [16384, 2048], P('ctx', 'head')
- grad_keys: bfloat16 [16384, 2048], P('ctx', 'head')
- grad_values: bfloat16 [16384, 2048], P('ctx', 'head')
All inputs are finite; a program needn't handle non-finite values.
Results may differ from a plain program's by a relative error of at most 0.008.
Values may be sent and summed in bfloat16 or wider, within the bound.
A program may use at most 128 MiB of HBM per device.

v0:
```python
import functools
import math

import jax
import jax.numpy as jnp
from jax import lax
from jax.experimental import pallas as pl
from jax.experimental.pallas import tpu as pltpu
from jax.sharding import PartitionSpec as P

B = 128
HEAD = 128
HALF = 512
HEADS = 4
KEYS = 1024
LOG_TWO = math.log(2.0)
LOG2E = 1.0 / LOG_TWO
ROOT = 1.0 / math.sqrt(HEAD)
F32 = jnp.float32
BF16 = jnp.bfloat16
MESH = pl.DeviceIdType.MESH

L1, L2, L3, L4, L5, L6 = 256, 384, 512, 640, 768, 896


def flip(index, bits):
    out = index
    for bit in bits:
        side = (index // (1 << bit)) % 2
        out = out + (1 - 2 * side) * (1 << bit)
    return out


def bits_of(mask, first):
    return [first + i for i in range(3) if mask >> i & 1]


def dot(a, b, dims=((1,), (0,))):
    return lax.dot_general(a, b, (dims, ((), ())), preferred_element_type=F32)


def pool_matrix(rows):
    r = lax.broadcasted_iota(jnp.int32, (rows // 2, rows), 0)
    c = lax.broadcasted_iota(jnp.int32, (rows // 2, rows), 1)
    return jnp.where(c // 2 == r, 0.5, 0.0).astype(BF16)


def pool(x):
    return dot(pool_matrix(x.shape[0]), x).astype(BF16)


def spread_matrix(rows, parts):
    blocks = []
    for ratio, width, copies in parts:
        r = lax.broadcasted_iota(jnp.int32, (rows, width * copies), 0)
        c = lax.broadcasted_iota(jnp.int32, (rows, width * copies), 1)
        blocks.append(jnp.where(r // ratio == c % width, 1.0 / ratio, 0.0).astype(BF16))
    return blocks


def kernel(
    slopes, q, k, v, g, w_hbm,
    layer_out, grad_q, grad_k, grad_v,
    kv, qc, gc, gfar, w, s1, s2, s3, a4, a5, a6, scores, gradw, prob, dsc,
    out, out3, back, g4, zin, acc, attn, whole, ga, send_part, recv_part, peer_q, peer_kv,
    send_sem, recv_sem, w_sem,
):
    ctx = lax.axis_index("ctx")
    head = lax.axis_index("head")
    core = ctx % 2
    mine = pl.ds(pl.multiple_of(core * HALF, HALF), HALF)
    theirs = pl.ds(pl.multiple_of((1 - core) * HALF, HALF), HALF)
    my_cols = pl.ds(pl.multiple_of(head * 1024, 1024), 1024)
    far_cols = pl.ds(pl.multiple_of((1 - head) * 1024, 1024), 1024)

    other = (flip(ctx, [0]), head)
    across = (ctx, 1 - head)
    z_peer = [None] + [(flip(ctx, bits_of(m, 1)), head) for m in range(1, 8)]
    xy_peer = [None] + [(flip(ctx, bits_of(m, 4)), head) for m in range(1, 8)]

    barrier = pltpu.get_barrier_semaphore()
    peers = [other, across] + z_peer[1:] + xy_peer[1:]
    for peer in peers:
        pl.semaphore_signal(barrier, inc=1, device_id=peer, device_id_type=MESH)

    load_w = pltpu.make_async_copy(w_hbm, w, w_sem)
    load_w.start()
    kv[0:128, 0:HALF] = k[:, mine]
    kv[0:128, HALF:1024] = v[:, mine]
    qc[0:128, :] = q[:, mine]

    pl.semaphore_wait(barrier, len(peers))

    count = [0]
    started = []

    def send(src, dst, peer):
        slot = count[0]
        count[0] += 1
        copy = pltpu.make_async_remote_copy(
            src_ref=src, dst_ref=dst, send_sem=send_sem.at[slot], recv_sem=recv_sem.at[slot],
            device_id=peer, device_id_type=MESH,
        )
        copy.start()
        started.append(copy)
        return copy

    in_k = send(k.at[:, theirs], kv.at[128:256, 0:HALF], other)
    in_v = send(v.at[:, theirs], kv.at[128:256, HALF:1024], other)
    in_g = send(g, gfar, across)
    in_q = send(q.at[:, theirs], qc.at[128:256, :], other)

    in_k.wait_recv()
    in_v.wait_recv()
    s1[...] = pool(kv[0:256, :])
    s2[...] = pool(s1[...])
    s3[...] = pool(s2[...])
    a4[0:16, :] = pool(s3[...])
    in3 = [send(s3, kv.at[L3 + 32 * (m - 4):L3 + 32 * (m - 3), :], z_peer[m]) for m in range(4, 8)]
    in4 = [send(a4.at[0:16, :], a4.at[16 * m:16 * (m + 1), :], z_peer[m]) for m in range(1, 4)]
    in2 = [send(s2, kv.at[L2 + 64 * (m - 2):L2 + 64 * (m - 1), :], z_peer[m]) for m in range(2, 4)]
    in1 = send(s1, kv.at[L1:L2, :], z_peer[1])

    load_w.wait()
    in_g.wait_recv()
    ga[...] = (
        dot(g[...], w[:, my_cols], ((1,), (1,))) + dot(gfar[...], w[:, far_cols], ((1,), (1,)))
    ).astype(BF16)
    gc[0:128, :] = ga[:, mine]
    in_ga = send(ga.at[:, theirs], gc.at[128:256, :], other)

    for copy in in3 + in4:
        copy.wait_recv()
    a4[64:128, :] = pool(kv[L3:L4, :])
    a5[...] = pool(a4[...])
    a6[...] = pool(a5[...])
    far4 = [send(a4, kv.at[L4:L5, :], xy_peer[1])]
    far5 = [send(a5, kv.at[L5 + 64 * (m - 2):L5 + 64 * (m - 1), :], xy_peer[m]) for m in range(2, 4)]
    far6 = [send(a6, kv.at[L6 + 32 * (m - 4):L6 + 32 * (m - 3), :], xy_peer[m]) for m in range(4, 8)]

    in_q.wait_recv()
    in_ga.wait_recv()

    def level_bias(h, level):
        slope = slopes[core * HEADS + h]
        return (level * LOG_TWO - slope * (level + 1.0)) * LOG2E

    def score_rows(h, low, high, bias):
        rows = slice(low, high)
        lanes = slice(h * HEAD, (h + 1) * HEAD)
        s = dot(kv[rows, lanes], qc[:, lanes], ((1,), (1,))) * (ROOT * LOG2E) + bias
        scores[h, rows, :] = s
        gradw[h, rows, :] = dot(
            kv[rows, HALF + h * HEAD:HALF + (h + 1) * HEAD], gc[:, lanes], ((1,), (1,))
        )
        return jnp.max(s, axis=0, keepdims=True)

    tops = []
    for h in range(HEADS):
        lane = lax.broadcasted_iota(jnp.int32, (1, 256), 1)
        bias = level_bias(h, 0)
        top = score_rows(h, 0, 128, jnp.where(lane < 128, 0.0, bias))
        top = jnp.maximum(top, score_rows(h, 128, 256, jnp.where(lane < 128, bias, 0.0)))
        tops.append(top)
    for level, low, copies in ((3, L3, []), (2, L2, in2), (1, L1, [in1])):
        for copy in copies:
            copy.wait_recv()
        for h in range(HEADS):
            tops[h] = jnp.maximum(tops[h], score_rows(h, low, low + 128, level_bias(h, level)))
    for level, low, copies in ((4, L4, far4), (5, L5, far5), (6, L6, far6)):
        for copy in copies:
            copy.wait_recv()
        for h in range(HEADS):
            tops[h] = jnp.maximum(tops[h], score_rows(h, low, low + 128, level_bias(h, level)))

    def gradients(h, low, high):
        lanes = slice(h * HEAD, (h + 1) * HEAD)
        d_key = dot(dsc[h, low:high, :], qc[:, lanes]) * ROOT
        d_value = dot(prob[h, low:high, :], gc[:, lanes])
        return d_key, d_value

    for h in range(HEADS):
        total = jnp.zeros((1, 256), F32)
        center = jnp.zeros((1, 256), F32)
        for low in range(0, KEYS, 128):
            e = jnp.exp2(scores[h, low:low + 128, :] - tops[h])
            scores[h, low:low + 128, :] = e
            total = total + jnp.sum(e, axis=0, keepdims=True)
            center = center + jnp.sum(e * gradw[h, low:low + 128, :], axis=0, keepdims=True)
        scale = 1.0 / total
        center = center * scale
        for low in range(0, KEYS, 128):
            weight = scores[h, low:low + 128, :] * scale
            prob[h, low:low + 128, :] = weight.astype(BF16)
            dsc[h, low:low + 128, :] = (weight * (gradw[h, low:low + 128, :] - center)).astype(BF16)
        d_key, d_value = gradients(h, L4, KEYS)
        out[L4 - 256:KEYS - 256, h * HEAD:(h + 1) * HEAD] = d_key.astype(BF16)
        out[L4 - 256:KEYS - 256, HALF + h * HEAD:HALF + (h + 1) * HEAD] = d_value.astype(BF16)

    def piece(low, rows):
        return out.at[low - 256:low - 256 + rows, :]

    back4 = [send(piece(L4, 128), back.at[0:128, :], xy_peer[1])]
    back4 += [
        send(piece(L5 + 64 * (m - 2), 64), back.at[128 + 64 * (m - 2):128 + 64 * (m - 1), :], xy_peer[m])
        for m in range(2, 4)
    ]
    back4 += [
        send(piece(L6 + 32 * (m - 4), 32), back.at[256 + 32 * (m - 4):256 + 32 * (m - 3), :], xy_peer[m])
        for m in range(4, 8)
    ]

    for h in range(HEADS):
        d_key, d_value = gradients(h, L1, L3)
        out[0:256, h * HEAD:(h + 1) * HEAD] = d_key.astype(BF16)
        out[0:256, HALF + h * HEAD:HALF + (h + 1) * HEAD] = d_value.astype(BF16)
    home = [
        send(piece(L2 + 64 * (m - 2), 64), zin.at[128 + 64 * (m - 2):128 + 64 * (m - 1), :], z_peer[m])
        for m in range(2, 4)
    ]
    home += [send(piece(L1, 128), zin.at[0:128, :], z_peer[1])]

    for h in range(HEADS):
        lanes = slice(h * HEAD, (h + 1) * HEAD)
        attn_t = dot(kv[:, HALF + h * HEAD:HALF + (h + 1) * HEAD], prob[h], ((0,), (0,)))
        both = attn_t.T.astype(BF16)
        whole[:, pl.ds(pl.multiple_of(core * HALF + h * HEAD, HEAD), HEAD)] = both[0:128]
        attn[:, lanes] = both[128:256]
    return_attn = send(attn, whole.at[:, mine], other)

    for h in range(HEADS):
        lanes = slice(h * HEAD, (h + 1) * HEAD)
        dq_t = dot(kv[:, lanes], dsc[h], ((0,), (0,))) * ROOT
        both = dq_t.T.astype(BF16)
        grad_q[:, pl.ds(pl.multiple_of(core * HALF + h * HEAD, HEAD), HEAD)] = both[0:128]
        peer_q[:, lanes] = both[128:256]
    return_q = send(peer_q, grad_q.at[:, mine], other)

    return_attn.wait_recv()
    send_part[...] = dot(whole[...], w[:, far_cols]).astype(BF16)
    part = send(send_part, recv_part, across)

    for h in range(HEADS):
        d_key, d_value = gradients(h, L3, L4)
        out3[:, h * HEAD:(h + 1) * HEAD] = d_key
        out3[:, HALF + h * HEAD:HALF + (h + 1) * HEAD] = d_value
        d_key, d_value = gradients(h, 0, 256)
        acc[:, h * HEAD:(h + 1) * HEAD] = d_key
        acc[:, HALF + h * HEAD:HALF + (h + 1) * HEAD] = d_value

    for copy in back4:
        copy.wait_recv()
    mix = spread_matrix(128, ((1, 128, 1), (2, 64, 2), (4, 32, 4)))
    folded = sum(dot(mix[i], back[128 * i:128 * (i + 1), :]) for i in range(3))
    g4[...] = folded.astype(BF16)
    zin[384:400, :] = g4[0:16, :]
    unpool = spread_matrix(128, ((2, 64, 1),))[0]
    out[L3 - 256:L4 - 256, :] = (out3[...] + dot(unpool, g4[64:128, :])).astype(BF16)
    home += [
        send(piece(L3 + 32 * (m - 4), 32), zin.at[256 + 32 * (m - 4):256 + 32 * (m - 3), :], z_peer[m])
        for m in range(4, 8)
    ]
    home += [
        send(g4.at[16 * m:16 * (m + 1), :], zin.at[384 + 16 * m:384 + 16 * (m + 1), :], z_peer[m])
        for m in range(1, 4)
    ]

    own_part = dot(whole[...], w[:, my_cols])
    part.wait_recv()
    layer_out[...] = (own_part + recv_part[...].astype(F32)).astype(BF16)

    for copy in home:
        copy.wait_recv()
    mix = spread_matrix(256, ((2, 128, 1), (4, 64, 2), (8, 32, 4), (16, 16, 4)))
    final = acc[...]
    for i in range(4):
        rows = slice(128 * i, min(128 * (i + 1), 448))
        final = final + dot(mix[i], zin[rows, :])
    done = final.astype(BF16)
    peer_kv[...] = done[128:256, :]
    return_k = send(peer_kv.at[:, 0:HALF], grad_k.at[:, mine], other)
    return_v = send(peer_kv.at[:, HALF:1024], grad_v.at[:, mine], other)
    grad_k[:, mine] = done[0:128, 0:HALF]
    grad_v[:, mine] = done[0:128, HALF:1024]
    return_q.wait_recv()
    return_k.wait_recv()
    return_v.wait_recv()
    for copy in started:
        copy.wait_send()


COPIES = 8 + 2 + 2 * (10 + 7)


def local(queries, key_vectors, value_vectors, slopes, w_out, grad_out):
    block = jax.ShapeDtypeStruct((B, 1024), BF16)
    vmem = pl.BlockSpec(memory_space=pltpu.VMEM)
    return pl.pallas_call(
        kernel,
        out_shape=[block] * 4,
        in_specs=[pl.BlockSpec(memory_space=pltpu.SMEM)] + [vmem] * 4 + [pl.BlockSpec(memory_space=pl.ANY)],
        out_specs=[vmem] * 4,
        scratch_shapes=[
            pltpu.VMEM((KEYS, 1024), BF16),
            pltpu.VMEM((256, HALF), BF16),
            pltpu.VMEM((256, HALF), BF16),
            pltpu.VMEM((128, 1024), BF16),
            pltpu.VMEM((1024, 2048), BF16),
            pltpu.VMEM((128, 1024), BF16),
            pltpu.VMEM((64, 1024), BF16),
            pltpu.VMEM((32, 1024), BF16),
            pltpu.VMEM((128, 1024), BF16),
            pltpu.VMEM((64, 1024), BF16),
            pltpu.VMEM((32, 1024), BF16),
            pltpu.VMEM((HEADS, KEYS, 256), F32),
            pltpu.VMEM((HEADS, KEYS, 256), F32),
            pltpu.VMEM((HEADS, KEYS, 256), BF16),
            pltpu.VMEM((HEADS, KEYS, 256), BF16),
            pltpu.VMEM((768, 1024), BF16),
            pltpu.VMEM((128, 1024), F32),
            pltpu.VMEM((384, 1024), BF16),
            pltpu.VMEM((128, 1024), BF16),
            pltpu.VMEM((448, 1024), BF16),
            pltpu.VMEM((256, 1024), F32),
            pltpu.VMEM((128, HALF), BF16),
            pltpu.VMEM((128, 1024), BF16),
            pltpu.VMEM((128, 1024), BF16),
            pltpu.VMEM((128, 1024), BF16),
            pltpu.VMEM((128, 1024), BF16),
            pltpu.VMEM((128, HALF), BF16),
            pltpu.VMEM((128, 1024), BF16),
            pltpu.SemaphoreType.DMA((COPIES,)),
            pltpu.SemaphoreType.DMA((COPIES,)),
            pltpu.SemaphoreType.DMA,
        ],
        compiler_params=pltpu.CompilerParams(
            collective_id=0, has_side_effects=True, vmem_limit_bytes=50 * 1024 * 1024
        ),
        cost_estimate=pl.CostEstimate(flops=2_700_000_000, bytes_accessed=8_000_000, transcendentals=1_000_000),
    )(slopes, queries, key_vectors, value_vectors, grad_out, w_out)


def solution(mesh):
    cut = P("ctx", "head")
    return jax.shard_map(
        local,
        mesh=mesh,
        in_specs=(cut, cut, cut, P("head"), P("head", None), cut),
        out_specs=(cut, cut, cut, cut),
        check_vma=False,
    )
```

profile of v0, /device:TPU:1, one launch (start us, length us, event | category | flops | bytes accessed | tf_op | source)
XLA Modules:
  0.0 76.7 jit_solution(11223361113129578165)
XLA Ops:
  0.6 0.0 copy-start
  0.6 0.9 %copy-done = bf16[128,1024]{1,0:T(8,128)(2,1)S(1)} copy-done((bf16[128,1024]{1,0:T(8,128)(2,1)S(1)}, bf16[128,1024]{1,0:T(8,128)(2,1)}, u32[]{:S(2)}) %copy-start) | copy-done | bytes 262168
  1.6 0.0 copy-start.1
  1.6 0.9 %copy-done.1 = bf16[128,1024]{1,0:T(8,128)(2,1)S(1)} copy-done((bf16[128,1024]{1,0:T(8,128)(2,1)S(1)}, bf16[128,1024]{1,0:T(8,128)(2,1)}, u32[]{:S(2)}) %copy-start.1) | copy-done | bytes 262168
  2.5 0.0 copy-start.2
  2.5 0.9 %copy-done.2 = bf16[128,1024]{1,0:T(8,128)(2,1)S(1)} copy-done((bf16[128,1024]{1,0:T(8,128)(2,1)S(1)}, bf16[128,1024]{1,0:T(8,128)(2,1)}, u32[]{:S(2)}) %copy-start.2) | copy-done | bytes 262168
  3.5 0.0 copy-start.3
  3.5 0.9 %copy-done.3 = bf16[128,1024]{1,0:T(8,128)(2,1)S(1)} copy-done((bf16[128,1024]{1,0:T(8,128)(2,1)S(1)}, bf16[128,1024]{1,0:T(8,128)(2,1)}, u32[]{:S(2)}) %copy-start.3) | copy-done | bytes 262168
  4.4 0.0 copy-start.4
  4.4 0.7 copy-done.4
  5.1 68.8 %shard_map.93 = (bf16[128,1024]{1,0:T(8,128)(2,1)S(1)}, bf16[128,1024]{1,0:T(8,128)(2,1)S(1)}, bf16[128,1024]{1,0:T(8,128)(2,1)S(1)}, bf16[128,1024]{1,0:T(8,128)(2,1)S(1)}) custom-call(f32[8]{0:T(128)S(1)} %copy-done.4, bf16[128,1024]{1,0:T(8,128)(2,1)S(1)} %copy-done, bf16[128,1024]{1,0:T(8,128)(2,1)S(1)} %copy-done.1, bf16[128,1024]{1,0:T(8,128)(2,1)S(1)} %copy-done.2, ...), custom_call_target="tpu_custom_call" | custom-call | flops 2700000000 | bytes 8000000 | tf_op jit(solution)/shard_map/pallas_call | solution.py:298
  73.9 0.7 copy.14
  74.6 0.7 copy.15
  75.3 0.7 copy.16
  76.0 0.7 copy.17
Async XLA Ops:
  0.6 1.0 %copy-start = (bf16[128,1024]{1,0:T(8,128)(2,1)S(1)}, bf16[128,1024]{1,0:T(8,128)(2,1)}, u32[]{:S(2)}) copy-start(bf16[128,1024]{1,0:T(8,128)(2,1)} %q.1) | copy-start | bytes 786436
  1.6 0.9 %copy-start.1 = (bf16[128,1024]{1,0:T(8,128)(2,1)S(1)}, bf16[128,1024]{1,0:T(8,128)(2,1)}, u32[]{:S(2)}) copy-start(bf16[128,1024]{1,0:T(8,128)(2,1)} %k.1) | copy-start | bytes 786436
  2.5 0.9 %copy-start.2 = (bf16[128,1024]{1,0:T(8,128)(2,1)S(1)}, bf16[128,1024]{1,0:T(8,128)(2,1)}, u32[]{:S(2)}) copy-start(bf16[128,1024]{1,0:T(8,128)(2,1)} %v.1) | copy-start | bytes 786436
  3.5 0.9 %copy-start.3 = (bf16[128,1024]{1,0:T(8,128)(2,1)S(1)}, bf16[128,1024]{1,0:T(8,128)(2,1)}, u32[]{:S(2)}) copy-start(bf16[128,1024]{1,0:T(8,128)(2,1)} %g.1) | copy-start | bytes 786436
  4.4 0.7 copy-start.4
where the time goes:
time: 77.1 us; the launch traced here: 76.7 us
  Pallas kernels  68.8 us (89%)
  local copies, waits for them, and re-layouts  7.26 us (9%)
    pallas_call x1, Pallas kernels, local(): pl.pallas_call(kernel, out_shape=[block] * 4, in_specs=[pl.BlockSpec(memo...  68.8 us
    unnamed x14, local copies, waits for them, and re-layouts  7.26 us

commit v1 on v0

v1 whole, which is shorter than its diff:
```python
import math

import jax
import jax.numpy as jnp
from jax import lax
from jax.experimental import pallas as pl
from jax.experimental.pallas import tpu as pltpu
from jax.sharding import PartitionSpec as P

B = 128
HEAD = 128
HALF = 512
HEADS = 4
KEYS = 1024
LOG_TWO = math.log(2.0)
LOG2E = 1.0 / LOG_TWO
ROOT = 1.0 / math.sqrt(HEAD)
F32 = jnp.float32
BF16 = jnp.bfloat16
MESH = pl.DeviceIdType.MESH

L1, L2, L3, L4, L5, L6 = 256, 384, 512, 640, 768, 896


def flip(index, bits):
    out = index
    for bit in bits:
        side = (index // (1 << bit)) % 2
        out = out + (1 - 2 * side) * (1 << bit)
    return out


def bits_of(mask, first):
    return [first + i for i in range(3) if mask >> i & 1]


def dot(a, b, dims=((1,), (0,))):
    return lax.dot_general(a, b, (dims, ((), ())), preferred_element_type=F32)


def grid_of(rows, columns):
    r = lax.broadcasted_iota(jnp.int32, (rows, columns), 0)
    c = lax.broadcasted_iota(jnp.int32, (rows, columns), 1)
    return r, c


def pool_f32(x):
    r, c = grid_of(x.shape[0] // 2, x.shape[0])
    return dot(jnp.where(c // 2 == r, 0.5, 0.0).astype(BF16), x)


def pool(x):
    return pool_f32(x).astype(BF16)


def spread(rows, parts):
    blocks = []
    for ratio, width, copies in parts:
        r, c = grid_of(rows, width * copies)
        blocks.append(jnp.where(r // ratio == c % width, 1.0 / ratio, 0.0).astype(BF16))
    return jnp.concatenate(blocks, axis=1)


def pack(x):
    return jnp.concatenate([x[:, 0:HALF], x[:, HALF:1024]], axis=0).astype(BF16)


def kernel(
    slopes_in, q, k, v, g, w_in,
    layer_out, grad_q, grad_k, grad_v,
    slopes, kv, kt, qc, gc, gown, gfar, w, s1, s2, s3, s4, packed, a4, a5, a6,
    scores, gradw, prob, dsc, out, out3, back, n4, zin, zin4, acc, acc_in,
    attn, whole, ga, send_part, recv_part, peer_q,
    send_sem, recv_sem, local_sem,
):
    ctx = lax.axis_index("ctx")
    head = lax.axis_index("head")
    core = ctx % 2
    mine = pl.ds(pl.multiple_of(core * HALF, HALF), HALF)
    theirs = pl.ds(pl.multiple_of((1 - core) * HALF, HALF), HALF)
    my_cols = pl.ds(pl.multiple_of(head * 1024, 1024), 1024)
    far_cols = pl.ds(pl.multiple_of((1 - head) * 1024, 1024), 1024)

    other = (flip(ctx, [0]), head)
    across = (ctx, 1 - head)
    z_peer = [[(flip(ctx, [0] * sub + bits_of(m, 1)), head) for sub in range(2)] for m in range(8)]
    xy_peer = [None] + [(flip(ctx, bits_of(m, 4)), head) for m in range(1, 8)]

    barrier = pltpu.get_barrier_semaphore()
    peers = [other, across] + sum(z_peer[1:], []) + xy_peer[1:]
    for peer in peers:
        pl.semaphore_signal(barrier, inc=1, device_id=peer, device_id_type=MESH)

    def load(src, dst, slot):
        copy = pltpu.make_async_copy(src, dst, local_sem.at[slot])
        copy.start()
        return copy

    load_kv = [
        load(k.at[:, mine], kv.at[0:128, 0:HALF], 0),
        load(v.at[:, mine], kv.at[0:128, HALF:1024], 1),
        load(k.at[:, theirs], kt.at[:, 0:HALF], 2),
        load(v.at[:, theirs], kt.at[:, HALF:1024], 3),
    ]
    load_rest = [
        load(q.at[:, mine], qc.at[0:128, :], 4),
        load(g, gown, 5),
        load(slopes_in, slopes, 6),
        load(w_in, w, 7),
    ]

    for copy in load_kv:
        copy.wait()
    for j, rows in ((0, kv[0:128, :]), (1, kt[...])):
        s1[j] = pool(rows)
        s2[j] = pool(s1[j])
        s3[j] = pool(s2[j])
        s4[j] = pack(pool_f32(s3[j]))
    packed[0:16, :] = s4[0]

    pl.semaphore_wait(barrier, len(peers))

    count = [0]
    started = []

    def send(src, dst, peer):
        slot = count[0]
        count[0] += 1
        copy = pltpu.make_async_remote_copy(
            src_ref=src, dst_ref=dst, send_sem=send_sem.at[slot], recv_sem=recv_sem.at[slot],
            device_id=peer, device_id_type=MESH,
        )
        copy.start()
        started.append(copy)
        return copy

    def packed_at(m, sub):
        return packed.at[32 * m + 16 * sub:32 * m + 16 * sub + 16, :]

    in4 = [send(s4.at[1], packed_at(0, 1), other)]
    in4 += [send(s4.at[sub], packed_at(m, sub), z_peer[m][sub]) for m in range(1, 4) for sub in range(2)]

    def z_sends(source, low, rows, masks):
        return [
            send(
                source.at[sub],
                kv.at[low + (2 * i + sub) * rows:low + (2 * i + sub + 1) * rows, :],
                z_peer[m][sub],
            )
            for i, m in enumerate(masks)
            for sub in range(2)
        ]

    in3 = z_sends(s3, L3, 16, (4, 5, 6, 7))
    in_kv = send(kt, kv.at[128:256, :], other)
    in_q = send(q.at[:, theirs], qc.at[128:256, :], other)
    in_g = send(g, gfar, across)
    in2 = z_sends(s2, L2, 32, (2, 3))
    in1 = z_sends(s1, L1, 64, (1,))

    def xy_sends(half):
        copies = [send(a4.at[64 * half:64 * half + 64, :], kv.at[L4 + 64 * half:L4 + 64 * half + 64, :], xy_peer[1])]
        for m in range(2, 4):
            low = L5 + 64 * (m - 2) + 32 * half
            copies.append(send(a5.at[32 * half:32 * half + 32, :], kv.at[low:low + 32, :], xy_peer[m]))
        for m in range(4, 8):
            low = L6 + 32 * (m - 4) + 16 * half
            copies.append(send(a6.at[16 * half:16 * half + 16, :], kv.at[low:low + 16, :], xy_peer[m]))
        return copies

    for copy in in4:
        copy.wait_recv()
    r, c = grid_of(64, 128)
    at_k = (r // 8) * 16 + r % 8
    a4[0:64, 0:HALF] = dot(jnp.where(c == at_k, 1.0, 0.0).astype(BF16), packed[...]).astype(BF16)
    a4[0:64, HALF:1024] = dot(jnp.where(c == at_k + 8, 1.0, 0.0).astype(BF16), packed[...]).astype(BF16)
    a5[0:32, :] = pool(a4[0:64, :])
    a6[0:16, :] = pool(a5[0:32, :])
    far = xy_sends(0)

    for copy in load_rest:
        copy.wait()
    in_g.wait_recv()
    ga[...] = (
        dot(gown[...], w[:, my_cols], ((1,), (1,))) + dot(gfar[...], w[:, far_cols], ((1,), (1,)))
    ).astype(BF16)
    gc[0:128, :] = ga[:, mine]
    in_ga = send(ga.at[:, theirs], gc.at[128:256, :], other)

    for copy in in3:
        copy.wait_recv()
    a4[64:128, :] = pool(kv[L3:L4, :])
    a5[32:64, :] = pool(a4[64:128, :])
    a6[16:32, :] = pool(a5[32:64, :])
    far += xy_sends(1)

    in_kv.wait_recv()
    in_q.wait_recv()
    in_ga.wait_recv()

    def level_bias(h, level):
        slope = slopes[core * HEADS + h]
        return (level * LOG_TWO - slope * (level + 1.0)) * LOG2E

    def score_rows(h, low, high, bias):
        rows = slice(low, high)
        lanes = slice(h * HEAD, (h + 1) * HEAD)
        s = dot(kv[rows, lanes], qc[:, lanes], ((1,), (1,))) * (ROOT * LOG2E) + bias
        scores[h, rows, :] = s
        gradw[h, rows, :] = dot(
            kv[rows, HALF + h * HEAD:HALF + (h + 1) * HEAD], gc[:, lanes], ((1,), (1,))
        )
        return jnp.max(s, axis=0, keepdims=True)

    tops = []
    for h in range(HEADS):
        lane = lax.broadcasted_iota(jnp.int32, (1, 256), 1)
        bias = level_bias(h, 0)
        top = score_rows(h, 0, 128, jnp.where(lane < 128, 0.0, bias))
        top = jnp.maximum(top, score_rows(h, 128, 256, jnp.where(lane < 128, bias, 0.0)))
        tops.append(top)
    for level, low, copies in ((3, L3, []), (2, L2, in2), (1, L1, in1), (4, L4, far), (5, L5, []), (6, L6, [])):
        for copy in copies:
            copy.wait_recv()
        for h in range(HEADS):
            tops[h] = jnp.maximum(tops[h], score_rows(h, low, low + 128, level_bias(h, level)))

    def gradients(h, low, high):
        lanes = slice(h * HEAD, (h + 1) * HEAD)
        d_key = dot(dsc[h, low:high, :], qc[:, lanes]) * ROOT
        d_value = dot(prob[h, low:high, :], gc[:, lanes])
        return d_key, d_value

    for h in range(HEADS):
        total = jnp.zeros((1, 256), F32)
        center = jnp.zeros((1, 256), F32)
        for low in range(0, KEYS, 128):
            e = jnp.exp2(scores[h, low:low + 128, :] - tops[h])
            scores[h, low:low + 128, :] = e
            total = total + jnp.sum(e, axis=0, keepdims=True)
            center = center + jnp.sum(e * gradw[h, low:low + 128, :], axis=0, keepdims=True)
        scale = 1.0 / total
        center = center * scale
        for low in range(0, KEYS, 128):
            weight = scores[h, low:low + 128, :] * scale
            prob[h, low:low + 128, :] = weight.astype(BF16)
            dsc[h, low:low + 128, :] = (weight * (gradw[h, low:low + 128, :] - center)).astype(BF16)
        d_key, d_value = gradients(h, L4, KEYS)
        out[L4 - 256:KEYS - 256, h * HEAD:(h + 1) * HEAD] = d_key.astype(BF16)
        out[L4 - 256:KEYS - 256, HALF + h * HEAD:HALF + (h + 1) * HEAD] = d_value.astype(BF16)

    def piece(low, rows):
        return out.at[low - 256:low - 256 + rows, :]

    def xy_back(half):
        copies = [send(piece(L4 + 64 * half, 64), back.at[half, 0:64, :], xy_peer[1])]
        for m in range(2, 4):
            at = 64 + 32 * (m - 2)
            copies.append(send(piece(L5 + 64 * (m - 2) + 32 * half, 32), back.at[half, at:at + 32, :], xy_peer[m]))
        for m in range(4, 8):
            at = 128 + 16 * (m - 4)
            copies.append(send(piece(L6 + 32 * (m - 4) + 16 * half, 16), back.at[half, at:at + 16, :], xy_peer[m]))
        return copies

    back_far = xy_back(1)
    back_near = xy_back(0)

    for h in range(HEADS):
        d_key, d_value = gradients(h, L1, L3)
        out[0:256, h * HEAD:(h + 1) * HEAD] = d_key.astype(BF16)
        out[0:256, HALF + h * HEAD:HALF + (h + 1) * HEAD] = d_value.astype(BF16)

    def z_back(low, rows, masks, at):
        return [
            send(
                piece(low + (2 * i + sub) * rows, rows),
                zin.at[sub, at + i * rows:at + (i + 1) * rows, :],
                z_peer[m][sub],
            )
            for i, m in enumerate(masks)
            for sub in range(2)
        ]

    home = z_back(L2, 32, (2, 3), 64) + z_back(L1, 64, (1,), 0)

    for h in range(HEADS):
        lanes = slice(h * HEAD, (h + 1) * HEAD)
        attn_t = dot(kv[:, HALF + h * HEAD:HALF + (h + 1) * HEAD], prob[h], ((0,), (0,)))
        both = attn_t.T.astype(BF16)
        whole[:, pl.ds(pl.multiple_of(core * HALF + h * HEAD, HEAD), HEAD)] = both[0:128]
        attn[:, lanes] = both[128:256]
    return_attn = send(attn, whole.at[:, mine], other)

    for h in range(HEADS):
        d_key, d_value = gradients(h, L3, L4)
        out3[:, h * HEAD:(h + 1) * HEAD] = d_key
        out3[:, HALF + h * HEAD:HALF + (h + 1) * HEAD] = d_value

    return_attn.wait_recv()
    send_part[...] = dot(whole[...], w[:, far_cols]).astype(BF16)
    part = send(send_part, recv_part, across)

    for copy in back_far:
        copy.wait_recv()
    mix = spread(128, ((2, 64, 1), (4, 32, 2), (8, 16, 4)))
    out[L3 - 256:L4 - 256, :] = (out3[...] + dot(mix, back[1])).astype(BF16)
    home += z_back(L3, 16, (4, 5, 6, 7), 128)

    for copy in back_near:
        copy.wait_recv()
    g4 = dot(spread(64, ((1, 64, 1), (2, 32, 2), (4, 16, 4))), back[0])
    for m in range(4):
        for sub in range(2):
            at = 16 * m + 8 * sub
            n4[2 * m + sub] = pack(g4[at:at + 8])
    zin4[0, 0:16, :] = n4[0]
    home += [send(n4.at[1], zin4.at[1, 0:16, :], other)]
    home += [
        send(n4.at[2 * m + sub], zin4.at[sub, 16 * m:16 * m + 16, :], z_peer[m][sub])
        for m in range(1, 4)
        for sub in range(2)
    ]

    for h in range(HEADS):
        d_key, d_value = gradients(h, 0, 256)
        acc[:, h * HEAD:(h + 1) * HEAD] = d_key
        acc[:, HALF + h * HEAD:HALF + (h + 1) * HEAD] = d_value
    home += [send(acc.at[128:256, :], acc_in, other)]

    for h in range(HEADS):
        lanes = slice(h * HEAD, (h + 1) * HEAD)
        dq_t = dot(kv[:, lanes], dsc[h], ((0,), (0,))) * ROOT
        both = dq_t.T.astype(BF16)
        grad_q[:, pl.ds(pl.multiple_of(core * HALF + h * HEAD, HEAD), HEAD)] = both[0:128]
        peer_q[:, lanes] = both[128:256]
    home += [send(peer_q, grad_q.at[:, mine], other)]

    own_part = dot(whole[...], w[:, my_cols])
    part.wait_recv()
    layer_out[...] = (own_part + recv_part[...].astype(F32)).astype(BF16)

    r, c = grid_of(128, 64)
    low_k = jnp.where(c % 16 == r // 16, 1.0 / 16, 0.0).astype(BF16)
    low_v = jnp.where(c % 16 == r // 16 + 8, 1.0 / 16, 0.0).astype(BF16)
    for copy in home:
        copy.wait_recv()
    for sub, base, cols in ((0, acc, mine), (1, acc_in, theirs)):
        total = base[0:128, :] + dot(mix, zin[sub])
        grad_k[:, cols] = (total[:, 0:HALF] + dot(low_k, zin4[sub])).astype(BF16)
        grad_v[:, cols] = (total[:, HALF:1024] + dot(low_v, zin4[sub])).astype(BF16)
    for copy in started:
        copy.wait_send()


COPIES = 9 + 2 + 2 * (20 + 14)


def store(*refs):
    sems = refs[8]
    copies = [pltpu.make_async_copy(refs[i], refs[4 + i], sems.at[i]) for i in range(4)]
    for copy in copies:
        copy.start()
    for copy in copies:
        copy.wait()


def local(queries, key_vectors, value_vectors, slopes, w_out, grad_out):
    block = jax.ShapeDtypeStruct((B, 1024), BF16)
    vmem = pl.BlockSpec(memory_space=pltpu.VMEM)
    anywhere = pl.BlockSpec(memory_space=pl.ANY)
    results = pl.pallas_call(
        kernel,
        out_shape=[block] * 4,
        in_specs=[pl.BlockSpec(memory_space=pltpu.HBM)] * 6,
        out_specs=[vmem] * 4,
        scratch_shapes=[
            pltpu.SMEM((8,), F32),
            pltpu.VMEM((KEYS, 1024), BF16),
            pltpu.VMEM((128, 1024), BF16),
            pltpu.VMEM((256, HALF), BF16),
            pltpu.VMEM((256, HALF), BF16),
            pltpu.VMEM((128, 1024), BF16),
            pltpu.VMEM((128, 1024), BF16),
            pltpu.VMEM((1024, 2048), BF16),
            pltpu.VMEM((2, 64, 1024), BF16),
            pltpu.VMEM((2, 32, 1024), BF16),
            pltpu.VMEM((2, 16, 1024), BF16),
            pltpu.VMEM((2, 16, HALF), BF16),
            pltpu.VMEM((128, HALF), BF16),
            pltpu.VMEM((128, 1024), BF16),
            pltpu.VMEM((64, 1024), BF16),
            pltpu.VMEM((32, 1024), BF16),
            pltpu.VMEM((HEADS, KEYS, 256), F32),
            pltpu.VMEM((HEADS, KEYS, 256), F32),
            pltpu.VMEM((HEADS, KEYS, 256), BF16),
            pltpu.VMEM((HEADS, KEYS, 256), BF16),
            pltpu.VMEM((768, 1024), BF16),
            pltpu.VMEM((128, 1024), F32),
            pltpu.VMEM((2, 192, 1024), BF16),
            pltpu.VMEM((8, 16, HALF), BF16),
            pltpu.VMEM((2, 192, 1024), BF16),
            pltpu.VMEM((2, 64, HALF), BF16),
            pltpu.VMEM((256, 1024), F32),
            pltpu.VMEM((128, 1024), F32),
            pltpu.VMEM((128, HALF), BF16),
            pltpu.VMEM((128, 1024), BF16),
            pltpu.VMEM((128, 1024), BF16),
            pltpu.VMEM((128, 1024), BF16),
            pltpu.VMEM((128, 1024), BF16),
            pltpu.VMEM((128, HALF), BF16),
            pltpu.SemaphoreType.DMA((COPIES,)),
            pltpu.SemaphoreType.DMA((COPIES,)),
            pltpu.SemaphoreType.DMA((8,)),
        ],
        compiler_params=pltpu.CompilerParams(
            collective_id=0, has_side_effects=True, vmem_limit_bytes=63 * 1024 * 1024
        ),
        cost_estimate=pl.CostEstimate(flops=2_700_000_000, bytes_accessed=8_000_000, transcendentals=1_000_000),
    )(slopes, queries, key_vectors, value_vectors, grad_out, w_out)
    return pl.pallas_call(
        store,
        out_shape=[block] * 4,
        in_specs=[vmem] * 4,
        out_specs=[pl.BlockSpec(memory_space=pltpu.HBM)] * 4,
        scratch_shapes=[pltpu.SemaphoreType.DMA((4,))],
    )(*results)


def solution(mesh):
    cut = P("ctx", "head")
    return jax.shard_map(
        local,
        mesh=mesh,
        in_specs=(cut, cut, cut, P("head"), P("head", None), cut),
        out_specs=(cut, cut, cut, cut),
        check_vma=False,
    )
```

time: 77.1 us -> 63.5 us (0.82)
  local copies, waits for them, and re-layouts: 7.26 us -> 0 us
  Pallas kernels: 68.8 us -> 62.8 us
    pallas_call x1, Pallas kernels: 68.8 us -> 60.6 us  [local(): pl.pallas_call(kernel, out_shape=[block] * 4, in_specs=[pl.BlockSpec(memo...]
    unnamed x14 -> x0, local copies, waits for them, and re-layouts: 7.26 us -> none
    pallas_call x0 -> x1, Pallas kernels: none -> 2.18 us  [local(): pl.pallas_call(store, out_shape=[block] * 4, in_specs=[vmem] * 4, out_spe...]
where the time goes in v1:
time: 63.5 us; the launch traced here: 63.4 us
  Pallas kernels  62.8 us (99%)
  between operations  0.64 us (1%)
    pallas_call x1, Pallas kernels, local(): pl.pallas_call(kernel, out_shape=[block] * 4, in_specs=[pl.BlockSpec(memo...  60.6 us
    pallas_call x1, Pallas kernels, local(): pl.pallas_call(store, out_shape=[block] * 4, in_specs=[vmem] * 4, out_spe...  2.18 us

profile of v1, /device:TPU:1, one launch (start us, length us, event | category | flops | bytes accessed | tf_op | source)
XLA Modules:
  0.0 63.4 jit_solution(377293412195601725)
XLA Ops:
  0.6 60.6 %shard_map.93 = (bf16[128,1024]{1,0:T(8,128)(2,1)}, bf16[128,1024]{1,0:T(8,128)(2,1)}, bf16[128,1024]{1,0:T(8,128)(2,1)}, bf16[128,1024]{1,0:T(8,128)(2,1)}) custom-call(f32[8]{0:T(128)} %slopes_in.1, bf16[128,1024]{1,0:T(8,128)(2,1)} %q.1, bf16[128,1024]{1,0:T(8,128)(2,1)} %k.1, bf16[128,1024]{1,0:T(8,128)(2,1)} %v.1, bf16[128,1024]{1,0:T(8,128)(2,1)} %g.1, ...), custom_call_target="tpu_custom_call" | custom-call | flops 2700000000 | bytes 8000000 | tf_op jit(solution)/shard_map/pallas_call | solution.py:371
  61.2 2.2 %shard_map.94 = (bf16[128,1024]{1,0:T(8,128)(2,1)}, bf16[128,1024]{1,0:T(8,128)(2,1)}, bf16[128,1024]{1,0:T(8,128)(2,1)}, bf16[128,1024]{1,0:T(8,128)(2,1)}) custom-call(bf16[128,1024]{1,0:T(8,128)(2,1)} %get-tuple-element.8.refs_0_, bf16[128,1024]{1,0:T(8,128)(2,1)} %get-tuple-element.9.refs_1_, bf16[128,1024]{1,0:T(8,128)(2,1)} %get-tuple-element.10.refs_2_, ...), custom_call_target="tpu_custom_call" | custom-call | tf_op jit(solution)/shard_map/pallas_call | solution.py:420

commit v2 on v1

--- a/solution.py
+++ b/solution.py
@@ -1,3 +1,4 @@
+import functools
 import math
 
 import jax
@@ -106,7 +107,6 @@
         load(q.at[:, mine], qc.at[0:128, :], 4),
         load(g, gown, 5),
         load(slopes_in, slopes, 6),
-        load(w_in, w, 7),
     ]
 
     for copy in load_kv:
@@ -116,6 +116,7 @@
         s2[j] = pool(s1[j])
         s3[j] = pool(s2[j])
         s4[j] = pack(pool_f32(s3[j]))
+    load_rest.append(load(w_in, w, 7))
     packed[0:16, :] = s4[0]
 
     pl.semaphore_wait(barrier, len(peers))
@@ -202,28 +203,68 @@
         slope = slopes[core * HEADS + h]
         return (level * LOG_TWO - slope * (level + 1.0)) * LOG2E
 
-    def score_rows(h, low, high, bias):
-        rows = slice(low, high)
+    def in_eights(x):
+        return x.reshape(x.shape[0] // 8, 8, 256)
+
+    def score_rows(h, low, bias):
+        rows = slice(low, low + 128)
         lanes = slice(h * HEAD, (h + 1) * HEAD)
         s = dot(kv[rows, lanes], qc[:, lanes], ((1,), (1,))) * (ROOT * LOG2E) + bias
         scores[h, rows, :] = s
         gradw[h, rows, :] = dot(
             kv[rows, HALF + h * HEAD:HALF + (h + 1) * HEAD], gc[:, lanes], ((1,), (1,))
         )
-        return jnp.max(s, axis=0, keepdims=True)
-
-    tops = []
-    for h in range(HEADS):
-        lane = lax.broadcasted_iota(jnp.int32, (1, 256), 1)
-        bias = level_bias(h, 0)
-        top = score_rows(h, 0, 128, jnp.where(lane < 128, 0.0, bias))
-        top = jnp.maximum(top, score_rows(h, 128, 256, jnp.where(lane < 128, bias, 0.0)))
-        tops.append(top)
-    for level, low, copies in ((3, L3, []), (2, L2, in2), (1, L1, in1), (4, L4, far), (5, L5, []), (6, L6, [])):
-        for copy in copies:
-            copy.wait_recv()
+        return jnp.max(in_eights(s), axis=0)
+
+    lane = lax.broadcasted_iota(jnp.int32, (1, 256), 1)
+
+    def bias_of(h, low):
+        if low < L1:
+            sibling = level_bias(h, 0)
+            return jnp.where((lane < 128) == (low == 0), 0.0, sibling)
+        return level_bias(h, {L1: 1, L2: 2, L3: 3, L4: 4, L5: 5, L6: 6}[low])
+
+    def group(lows):
+        stats = []
         for h in range(HEADS):
-            tops[h] = jnp.maximum(tops[h], score_rows(h, low, low + 128, level_bias(h, level)))
+            top = functools.reduce(jnp.maximum, [score_rows(h, low, bias_of(h, low)) for low in lows])
+            top = jnp.max(top, axis=0, keepdims=True)
+            total = jnp.zeros((8, 256), F32)
+            center = jnp.zeros((8, 256), F32)
+            for low in lows:
+                e = jnp.exp2(scores[h, low:low + 128, :] - top)
+                scores[h, low:low + 128, :] = e
+                total = total + jnp.sum(in_eights(e), axis=0)
+                center = center + jnp.sum(in_eights(e * gradw[h, low:low + 128, :]), axis=0)
+            stats.append((top, jnp.sum(total, axis=0, keepdims=True), jnp.sum(center, axis=0, keepdims=True)))
+        return stats
+
+    near_lows, mid_lows, far_lows = (0, 128, L3), (L2, L1), (L4, L5, L6)
+    groups = [group(near_lows)]
+    for copy in in2 + in1:
+        copy.wait_recv()
+    groups.append(group(mid_lows))
+    for copy in far:
+        copy.wait_recv()
+    groups.append(group(far_lows))
+
+    scales = []
+    centers = []
+    for h in range(HEADS):
+        tops = [stats[h][0] for stats in groups]
+        best = functools.reduce(jnp.maximum, tops)
+        factors = [jnp.exp2(top - best) for top in tops]
+        total = sum(f * stats[h][1] for f, stats in zip(factors, groups))
+        center = sum(f * stats[h][2] for f, stats in zip(factors, groups))
+        inverse = 1.0 / total
+        scales.append([f * inverse for f in factors])
+        centers.append(center * inverse)
+
+    def normalise(h, index, lows):
+        for low in lows:
+            weight = scores[h, low:low + 128, :] * scales[h][index]
+            prob[h, low:low + 128, :] = weight.astype(BF16)
+            dsc[h, low:low + 128, :] = (weight * (gradw[h, low:low + 128, :] - centers[h])).astype(BF16)
 
     def gradients(h, low, high):
         lanes = slice(h * HEAD, (h + 1) * HEAD)
@@ -231,23 +272,14 @@
         d_value = dot(prob[h, low:high, :], gc[:, lanes])
         return d_key, d_value
 
-    for h in range(HEADS):
-        total = jnp.zeros((1, 256), F32)
-        center = jnp.zeros((1, 256), F32)
-        for low in range(0, KEYS, 128):
-            e = jnp.exp2(scores[h, low:low + 128, :] - tops[h])
-            scores[h, low:low + 128, :] = e
-            total = total + jnp.sum(e, axis=0, keepdims=True)
-            center = center + jnp.sum(e * gradw[h, low:low + 128, :], axis=0, keepdims=True)
-        scale = 1.0 / total
-        center = center * scale
-        for low in range(0, KEYS, 128):
-            weight = scores[h, low:low + 128, :] * scale
-            prob[h, low:low + 128, :] = weight.astype(BF16)
-            dsc[h, low:low + 128, :] = (weight * (gradw[h, low:low + 128, :] - center)).astype(BF16)
-        d_key, d_value = gradients(h, L4, KEYS)
-        out[L4 - 256:KEYS - 256, h * HEAD:(h + 1) * HEAD] = d_key.astype(BF16)
-        out[L4 - 256:KEYS - 256, HALF + h * HEAD:HALF + (h + 1) * HEAD] = d_value.astype(BF16)
+    def put(h, low, high):
+        d_key, d_value = gradients(h, low, high)
+        out[low - 256:high - 256, h * HEAD:(h + 1) * HEAD] = d_key.astype(BF16)
+        out[low - 256:high - 256, HALF + h * HEAD:HALF + (h + 1) * HEAD] = d_value.astype(BF16)
+
+    for h in range(HEADS):
+        normalise(h, 2, far_lows)
+        put(h, L4, KEYS)
 
     def piece(low, rows):
         return out.at[low - 256:low - 256 + rows, :]
@@ -266,9 +298,8 @@
     back_near = xy_back(0)
 
     for h in range(HEADS):
-        d_key, d_value = gradients(h, L1, L3)
-        out[0:256, h * HEAD:(h + 1) * HEAD] = d_key.astype(BF16)
-        out[0:256, HALF + h * HEAD:HALF + (h + 1) * HEAD] = d_value.astype(BF16)
+        normalise(h, 1, mid_lows)
+        put(h, L1, L3)
 
     def z_back(low, rows, masks, at):
         return [
@@ -284,6 +315,7 @@
     home = z_back(L2, 32, (2, 3), 64) + z_back(L1, 64, (1,), 0)
 
     for h in range(HEADS):
+        normalise(h, 0, near_lows)
         lanes = slice(h * HEAD, (h + 1) * HEAD)
         attn_t = dot(kv[:, HALF + h * HEAD:HALF + (h + 1) * HEAD], prob[h], ((0,), (0,)))
         both = attn_t.T.astype(BF16)
@@ -370,7 +402,7 @@
     anywhere = pl.BlockSpec(memory_space=pl.ANY)
     results = pl.pallas_call(
         kernel,
-        out_shape=[block] * 4,
+        out_shape=[pltpu.VMEM((B, 1024), BF16)] * 4,
         in_specs=[pl.BlockSpec(memory_space=pltpu.HBM)] * 6,
         out_specs=[vmem] * 4,
         scratch_shapes=[
@@ -413,17 +445,17 @@
             pltpu.SemaphoreType.DMA((8,)),
         ],
         compiler_params=pltpu.CompilerParams(
-            collective_id=0, has_side_effects=True, vmem_limit_bytes=63 * 1024 * 1024
+            collective_id=0, has_side_effects=True, vmem_limit_bytes=48 * 1024 * 1024
         ),
         cost_estimate=pl.CostEstimate(flops=2_700_000_000, bytes_accessed=8_000_000, transcendentals=1_000_000),
-    )(slopes, queries, key_vectors, value_vectors, grad_out, w_out)
+    )(*(pltpu.with_memory_space_constraint(x, pltpu.HBM) for x in (slopes, queries, key_vectors, value_vectors, grad_out, w_out)))
     return pl.pallas_call(
         store,
         out_shape=[block] * 4,
         in_specs=[vmem] * 4,
         out_specs=[pl.BlockSpec(memory_space=pltpu.HBM)] * 4,
         scratch_shapes=[pltpu.SemaphoreType.DMA((4,))],
-    )(*results)
+    )(*(pltpu.with_memory_space_constraint(x, pltpu.VMEM) for x in results))
 
 
 def solution(mesh):

time: 63.5 us -> 60.7 us (0.956)
  Pallas kernels: 62.8 us -> 59.9 us
    pallas_call x1, Pallas kernels: 60.6 us -> 58.9 us  [local(): pl.pallas_call(kernel, out_shape=[pltpu.VMEM((B, 1024), BF16)] * 4, in_sp...]
    pallas_call x1, Pallas kernels: 2.18 us -> 1 us  [local(): pl.pallas_call(store, out_shape=[block] * 4, in_specs=[vmem] * 4, out_spe...]
where the time goes in v2:
time: 60.7 us; the launch traced here: 60.6 us
  Pallas kernels  59.9 us (99%)
  between operations  0.64 us (1%)
    pallas_call x1, Pallas kernels, local(): pl.pallas_call(kernel, out_shape=[pltpu.VMEM((B, 1024), BF16)] * 4, in_sp...  58.9 us

profile of v2, /device:TPU:1, one launch (start us, length us, event | category | flops | bytes accessed | tf_op | source)
XLA Modules:
  0.0 60.6 jit_solution(2776554313146879665)
XLA Ops:
  0.6 58.9 %shard_map.93 = (bf16[128,1024]{1,0:T(8,128)(2,1)S(1)}, bf16[128,1024]{1,0:T(8,128)(2,1)S(1)}, bf16[128,1024]{1,0:T(8,128)(2,1)S(1)}, bf16[128,1024]{1,0:T(8,128)(2,1)S(1)}) custom-call(f32[8]{0:T(128)} %slopes_in.1, bf16[128,1024]{1,0:T(8,128)(2,1)} %q.1, bf16[128,1024]{1,0:T(8,128)(2,1)} %k.1, bf16[128,1024]{1,0:T(8,128)(2,1)} %v.1, bf16[128,1024]{1,0:T(8,128)(2,1)} %g.1, ...), custom_call_target="tpu_custom_call" | custom-call | flops 2700000000 | bytes 8000000 | tf_op jit(solution)/shard_map/pallas_call | solution.py:403
  59.6 1.0 %shard_map.94 = (bf16[128,1024]{1,0:T(8,128)(2,1)}, bf16[128,1024]{1,0:T(8,128)(2,1)}, bf16[128,1024]{1,0:T(8,128)(2,1)}, bf16[128,1024]{1,0:T(8,128)(2,1)}) custom-call(bf16[128,1024]{1,0:T(8,128)(2,1)S(1)} %get-tuple-element.8.refs_0_, bf16[128,1024]{1,0:T(8,128)(2,1)S(1)} %get-tuple-element.9.refs_1_, bf16[128,1024]{1,0:T(8,128)(2,1)S(1)} %get-tuple-element.10.refs_2_, ...), custom_call_target="tpu_custom_call" | custom-call | tf_op jit(solution)/shard_map/pallas_call | solution.py:452

commit v3 on v1

v3 whole, which is shorter than its diff:
```python
import functools
import math

import jax
import jax.numpy as jnp
from jax import lax
from jax.experimental import pallas as pl
from jax.experimental.pallas import tpu as pltpu
from jax.sharding import PartitionSpec as P

B = 128
HEAD = 128
HEADS = 2
QUARTER = 256
LANES = 512
LOG_TWO = math.log(2.0)
LOG2E = 1.0 / LOG_TWO
ROOT = 1.0 / math.sqrt(HEAD)
F32 = jnp.float32
BF16 = jnp.bfloat16
MESH = pl.DeviceIdType.MESH

L1, L2, L3, L4, L5, L6, ROWS = 512, 768, 896, 1024, 1152, 1280, 1408
S1, S2, S3, S4, S5, S6, KEYS = 256, 384, 512, 640, 768, 896, 1024


def flip(index, bits):
    out = index
    for bit in bits:
        side = (index // (1 << bit)) % 2
        out = out + (1 - 2 * side) * (1 << bit)
    return out


def bits_of(mask, first):
    return [first + i for i in range(3) if mask >> i & 1]


def dot(a, b, dims=((1,), (0,))):
    return lax.dot_general(a, b, (dims, ((), ())), preferred_element_type=F32)


def grid_of(rows, columns):
    r = lax.broadcasted_iota(jnp.int32, (rows, columns), 0)
    c = lax.broadcasted_iota(jnp.int32, (rows, columns), 1)
    return r, c


def pools(rows, ratios):
    blocks = []
    for ratio in ratios:
        r, c = grid_of(rows // ratio, rows)
        blocks.append(jnp.where(c // ratio == r, 1.0 / ratio, 0.0).astype(BF16))
    return jnp.concatenate(blocks, axis=0)


def spread(rows, parts):
    blocks = []
    for ratio, width, copies in parts:
        r, c = grid_of(rows, width * copies)
        blocks.append(jnp.where(r // ratio == c % width, 1.0 / ratio, 0.0).astype(BF16))
    return jnp.concatenate(blocks, axis=1)


def pack(x):
    return jnp.concatenate([x[:, 0:QUARTER], x[:, QUARTER:LANES]], axis=0).astype(BF16)


def in_eights(x):
    return x.reshape(x.shape[0] // 8, 8, x.shape[1])


def kernel(
    slopes_in, q, k, v, g, w_in,
    layer_out, grad_q, grad_k, grad_v,
    slopes, kv, kt, qc, gc, gown, gfar, w, s2, s3, s4, packed, a4, a5, a6,
    scores, gradw, prob, dsc, out, out3, back, n4, zin, zin4, acc, acc_core, acc_out, acc_mate,
    attn, whole, ga, send_part, recv_part, dq,
    send_sem, recv_sem, local_sem,
):
    ctx = lax.axis_index("ctx")
    head = lax.axis_index("head")
    core = ctx % 2
    place = (ctx // 2) % 2

    def cols(j):
        a, c = j // 2, j % 2
        number = (place + a - 2 * place * a) * 2 + (core + c - 2 * core * c)
        return pl.ds(pl.multiple_of(number * QUARTER, QUARTER), QUARTER)

    my_cols = pl.ds(pl.multiple_of(head * 1024, 1024), 1024)
    far_cols = pl.ds(pl.multiple_of((1 - head) * 1024, 1024), 1024)

    across = (ctx, 1 - head)
    z_peer = [[(flip(ctx, [0] * sub + bits_of(m, 1)), head) for sub in range(2)] for m in range(8)]
    other = z_peer[0][1]
    xy_peer = [None] + [(flip(ctx, bits_of(m, 4)), head) for m in range(1, 8)]

    def load(src, dst, slot):
        copy = pltpu.make_async_copy(src, dst, local_sem.at[slot])
        copy.start()
        return copy

    load_kv = []
    for j in range(4):
        into = kv.at[0:128, :] if j == 0 else kt.at[128 * (j - 1):128 * j, :]
        load_kv.append(load(k.at[:, cols(j)], into.at[:, 0:QUARTER], 2 * j))
        load_kv.append(load(v.at[:, cols(j)], into.at[:, QUARTER:LANES], 2 * j + 1))

    barrier = pltpu.get_barrier_semaphore()
    peers = [other, across] + sum(z_peer[1:], []) + xy_peer[1:]
    for peer in peers:
        pl.semaphore_signal(barrier, inc=1, device_id=peer, device_id_type=MESH)

    load_rest = [
        load(q.at[:, cols(0)], qc.at[0:128, :], 8),
        load(g, gown, 9),
        load(slopes_in, slopes, 10),
    ]
    for copy in load_kv:
        copy.wait()
    means = pools(128, (4, 8, 16))
    for j in range(4):
        pooled = dot(means, kv[0:128, :] if j == 0 else kt[128 * (j - 1):128 * j, :])
        s2[j] = pooled[0:32].astype(BF16)
        s3[j] = pooled[32:48].astype(BF16)
        s4[j] = pack(pooled[48:56])
    packed[0:16, :] = s4[0]
    load_rest.append(load(w_in, w, 11))

    pl.semaphore_wait(barrier, len(peers))

    count = [0]
    started = []

    def send(src, dst, peer):
        slot = count[0]
        count[0] += 1
        copy = pltpu.make_async_remote_copy(
            src_ref=src, dst_ref=dst, send_sem=send_sem.at[slot], recv_sem=recv_sem.at[slot],
            device_id=peer, device_id_type=MESH,
        )
        copy.start()
        started.append(copy)
        return copy

    def packed_at(m, sub):
        return packed.at[32 * m + 16 * sub:32 * m + 16 * sub + 16, :]

    in4 = [send(s4.at[1], packed_at(0, 1), other)]
    in4 += [
        send(s4.at[2 * (m % 2) + sub], packed_at(m, sub), z_peer[m][sub])
        for m in range(1, 4) for sub in range(2)
    ]

    def z_sends(source, low, rows, masks):
        return [
            send(
                source.at[2 * (m % 2) + sub],
                kv.at[low + (2 * i + sub) * rows:low + (2 * i + sub + 1) * rows, :],
                z_peer[m][sub],
            )
            for i, m in enumerate(masks)
            for sub in range(2)
        ]

    pair_peer = [None, other, z_peer[1][0], z_peer[1][1]]

    def at_pair(ref, j):
        return ref.at[128 * j:128 * j + 128, :]

    in3 = z_sends(s3, L3, 16, (4, 5, 6, 7))
    in_g = send(g, gfar, across)
    in_kv = [send(kt.at[0:128, :], at_pair(kv, 1), other)]
    in_q = [send(q.at[:, cols(j)], at_pair(qc, j), pair_peer[j]) for j in range(1, 4)]
    in2 = z_sends(s2, L2, 32, (2, 3))

    def xy_sends(half):
        copies = [send(a4.at[64 * half:64 * half + 64, :], kv.at[L4 + 64 * half:L4 + 64 * half + 64, :], xy_peer[1])]
        for m in range(2, 4):
            low = L5 + 64 * (m - 2) + 32 * half
            copies.append(send(a5.at[32 * half:32 * half + 32, :], kv.at[low:low + 32, :], xy_peer[m]))
        for m in range(4, 8):
            low = L6 + 32 * (m - 4) + 16 * half
            copies.append(send(a6.at[16 * half:16 * half + 16, :], kv.at[low:low + 16, :], xy_peer[m]))
        return copies

    for copy in in4:
        copy.wait_recv()
    r, c = grid_of(64, 128)
    at_k = (r // 8) * 16 + r % 8
    halves = pools(64, (2, 4))
    a4[0:64, 0:QUARTER] = dot(jnp.where(c == at_k, 1.0, 0.0).astype(BF16), packed[...]).astype(BF16)
    a4[0:64, QUARTER:LANES] = dot(jnp.where(c == at_k + 8, 1.0, 0.0).astype(BF16), packed[...]).astype(BF16)
    upper = dot(halves, a4[0:64, :]).astype(BF16)
    a5[0:32, :] = upper[0:32]
    a6[0:16, :] = upper[32:48]
    far = xy_sends(0)

    for copy in in3:
        copy.wait_recv()
    upper = dot(pools(128, (2, 4, 8)), kv[L3:L4, :]).astype(BF16)
    a4[64:128, :] = upper[0:64]
    a5[32:64, :] = upper[64:96]
    a6[16:32, :] = upper[96:112]
    far += xy_sends(1)

    for copy in load_rest:
        copy.wait()
    in_g.wait_recv()
    ga[...] = (
        dot(gown[...], w[:, my_cols], ((1,), (1,))) + dot(gfar[...], w[:, far_cols], ((1,), (1,)))
    ).astype(BF16)
    gc[0:128, :] = ga[:, cols(0)]
    in_ga = [send(ga.at[:, cols(j)], at_pair(gc, j), pair_peer[j]) for j in range(1, 4)]
    in_kv += [send(kt.at[128 * (j - 1):128 * j, :], at_pair(kv, j), pair_peer[j]) for j in range(2, 4)]

    lane = lax.broadcasted_iota(jnp.int32, (1, 256), 1)

    def level_bias(h, level):
        slope = slopes[(place * 2 + core) * HEADS + h]
        return (level * LOG_TWO - slope * (level + 1.0)) * LOG2E

    def bias_of(h, at):
        if at < S1:
            return jnp.where((lane < 128) == (at == 0), 0.0, level_bias(h, 0))
        return level_bias(h, {S1: 1, S2: 2, S3: 3, S4: 4, S5: 5, S6: 6}[at])

    def key_row(chip, at):
        if at < S1:
            return 256 * chip + at
        if at < S2:
            return L1 + 128 * (1 - chip) + at - S1
        return L2 + at - S2

    def key_lanes(h):
        return slice(h * HEAD, (h + 1) * HEAD)

    def value_lanes(h):
        return slice(QUARTER + h * HEAD, QUARTER + (h + 1) * HEAD)

    def queries_of(chip):
        return slice(256 * chip, 256 * chip + 256)

    def score_rows(h, chip, at):
        row = key_row(chip, at)
        rows, own = slice(row, row + 128), queries_of(chip)
        s = dot(kv[rows, key_lanes(h)], qc[own, key_lanes(h)], ((1,), (1,))) * (ROOT * LOG2E) + bias_of(h, at)
        scores[h, at:at + 128, own] = s
        gradw[h, at:at + 128, own] = dot(kv[rows, value_lanes(h)], gc[own, key_lanes(h)], ((1,), (1,)))
        return jnp.max(in_eights(s), axis=0)

    units = [(h, chip) for chip in range(2) for h in range(HEADS)]
    stats = {unit: [] for unit in units}
    group_of = {unit: {} for unit in units}

    def group(unit, places):
        h, chip = unit
        own = queries_of(chip)
        top = functools.reduce(jnp.maximum, [score_rows(h, chip, at) for at in places])
        top = jnp.max(top, axis=0, keepdims=True)
        total = jnp.zeros((8, 256), F32)
        center = jnp.zeros((8, 256), F32)
        for at in places:
            e = jnp.exp2(scores[h, at:at + 128, own] - top)
            scores[h, at:at + 128, own] = e
            total = total + jnp.sum(in_eights(e), axis=0)
            center = center + jnp.sum(in_eights(e * gradw[h, at:at + 128, own]), axis=0)
            group_of[unit][at] = len(stats[unit])
        stats[unit].append((top, jnp.sum(total, axis=0, keepdims=True), jnp.sum(center, axis=0, keepdims=True)))

    for copy in in_kv[:1] + in_q + in2 + far + in_ga:
        copy.wait_recv()
    for unit in units[0:2]:
        group(unit, (0, 128, S2, S3, S4, S5, S6))
    for unit in units[2:4]:
        group(unit, (S2, S3, S4, S5, S6))
    for copy in in_kv[1:]:
        copy.wait_recv()
    twos = pools(256, (2,))
    for chip in range(2):
        kv[L1 + 128 * chip:L1 + 128 * chip + 128, :] = dot(twos, kv[256 * chip:256 * chip + 256, :]).astype(BF16)
    for unit in units[0:2]:
        group(unit, (S1,))
    for unit in units[2:4]:
        group(unit, (0, 128, S1))

    scales, centers = {}, {}
    for unit in units:
        tops = [stat[0] for stat in stats[unit]]
        best = functools.reduce(jnp.maximum, tops)
        factors = [jnp.exp2(top - best) for top in tops]
        inverse = 1.0 / sum(f * stat[1] for f, stat in zip(factors, stats[unit]))
        centers[unit] = sum(f * stat[2] for f, stat in zip(factors, stats[unit])) * inverse
        scales[unit] = [f * inverse for f in factors]

    def normalise(h, places):
        for chip in range(2):
            own = queries_of(chip)
            for at in places:
                weight = scores[h, at:at + 128, own] * scales[h, chip][group_of[h, chip][at]]
                prob[h, at:at + 128, own] = weight.astype(BF16)
                dsc[h, at:at + 128, own] = (weight * (gradw[h, at:at + 128, own] - centers[h, chip])).astype(BF16)

    def gradients(h, low, high):
        d_key = dot(dsc[h, low:high, :], qc[:, key_lanes(h)]) * ROOT
        d_value = dot(prob[h, low:high, :], gc[:, key_lanes(h)])
        return d_key, d_value

    def put(h, low, high):
        d_key, d_value = gradients(h, low, high)
        out[low - S2:high - S2, key_lanes(h)] = d_key.astype(BF16)
        out[low - S2:high - S2, value_lanes(h)] = d_value.astype(BF16)

    def piece(low, rows):
        return out.at[low - S2:low - S2 + rows, :]

    for h in range(HEADS):
        normalise(h, (S4, S5, S6))
        put(h, S4, KEYS)

    def xy_back(half):
        copies = [send(piece(S4 + 64 * half, 64), back.at[half, 0:64, :], xy_peer[1])]
        for m in range(2, 4):
            at = 64 + 32 * (m - 2)
            copies.append(send(piece(S5 + 64 * (m - 2) + 32 * half, 32), back.at[half, at:at + 32, :], xy_peer[m]))
        for m in range(4, 8):
            at = 128 + 16 * (m - 4)
            copies.append(send(piece(S6 + 32 * (m - 4) + 16 * half, 16), back.at[half, at:at + 16, :], xy_peer[m]))
        return copies

    back_far = xy_back(1)
    back_near = xy_back(0)

    for h in range(HEADS):
        normalise(h, (S2,))
        put(h, S2, S3)
    home = [
        send(piece(S2 + (2 * i + sub) * 32, 32), zin.at[2 * (m % 2) + sub, 0:32, :], z_peer[m][sub])
        for i, m in enumerate((2, 3))
        for sub in range(2)
    ]

    for h in range(HEADS):
        normalise(h, (0, 128, S1, S3))
        d_key, d_value = gradients(h, S3, S4)
        out3[:, key_lanes(h)] = d_key
        out3[:, value_lanes(h)] = d_value

    def to_queries(h, lanes, weights):
        both = []
        for chip in range(2):
            own = queries_of(chip)
            level1 = key_row(chip, S1)
            total = (
                dot(kv[L2:ROWS, lanes], weights[h, S2:KEYS, own], ((0,), (0,)))
                + dot(kv[256 * chip:256 * chip + 256, lanes], weights[h, 0:S1, own], ((0,), (0,)))
                + dot(kv[level1:level1 + 128, lanes], weights[h, S1:S2, own], ((0,), (0,)))
            )
            both.append(total.T)
        return both

    for h in range(HEADS):
        for chip, part in enumerate(to_queries(h, value_lanes(h), prob)):
            attn[queries_of(chip), key_lanes(h)] = part.astype(BF16)
    whole[:, cols(0)] = attn[0:128, :]
    return_attn = [send(at_pair(attn, j), whole.at[:, cols(0)], pair_peer[j]) for j in (2, 3, 1)]

    for copy in back_far:
        copy.wait_recv()
    mix = spread(128, ((2, 64, 1), (4, 32, 2), (8, 16, 4)))
    out[S3 - S2:S4 - S2, :] = (out3[...] + dot(mix, back[1])).astype(BF16)
    home += [
        send(
            piece(S3 + (2 * i + sub) * 16, 16),
            zin.at[2 * (m % 2) + sub, 32 + 16 * (i // 2):48 + 16 * (i // 2), :],
            z_peer[m][sub],
        )
        for i, m in enumerate((4, 5, 6, 7))
        for sub in range(2)
    ]

    double = spread(256, ((2, 128, 1),))
    for h in range(HEADS):
        for chip in range(2):
            own, theirs = queries_of(chip), queries_of(1 - chip)
            for weights, by, lanes, factor in ((dsc, qc, key_lanes(h), ROOT), (prob, gc, value_lanes(h), 1.0)):
                level1 = dot(double, weights[h, S1:S2, theirs]).astype(BF16)
                total = dot(weights[h, 0:S1, own], by[own, key_lanes(h)]) + dot(level1, by[theirs, key_lanes(h)])
                acc[own, lanes] = total * factor
    acc_out[...] = acc[256:512, :].astype(BF16)
    home += [send(acc.at[128:256, :], acc_core, other)]
    home += [send(acc_out.at[128 * i:128 * i + 128, :], acc_mate.at[128 * i:128 * i + 128, :], pair_peer[2 + i]) for i in range(2)]

    for copy in back_near:
        copy.wait_recv()
    g4 = dot(spread(64, ((1, 64, 1), (2, 32, 2), (4, 16, 4))), back[0])
    for m in range(4):
        for sub in range(2):
            at = 16 * m + 8 * sub
            n4[2 * m + sub] = pack(g4[at:at + 8])
    zin4[0, 0:16, :] = n4[0]
    home += [send(n4.at[1], zin4.at[1, 0:16, :], other)]
    home += [
        send(n4.at[2 * m + sub], zin4.at[2 * (m % 2) + sub, 16 * (m // 2):16 * (m // 2) + 16, :], z_peer[m][sub])
        for m in range(1, 4)
        for sub in range(2)
    ]

    for h in range(HEADS):
        for chip, part in enumerate(to_queries(h, key_lanes(h), dsc)):
            dq[queries_of(chip), key_lanes(h)] = (part * ROOT).astype(BF16)
    grad_q[:, cols(0)] = dq[0:128, :]
    home += [send(at_pair(dq, j), grad_q.at[:, cols(0)], pair_peer[j]) for j in (2, 3, 1)]

    for copy in return_attn:
        copy.wait_recv()
    send_part[...] = dot(whole[...], w[:, far_cols]).astype(BF16)
    part = send(send_part, recv_part, across)
    own_part = dot(whole[...], w[:, my_cols])
    part.wait_recv()
    layer_out[...] = (own_part + recv_part[...].astype(F32)).astype(BF16)

    mix = spread(128, ((4, 32, 1), (8, 16, 2)))
    r, c = grid_of(128, 32)
    low_k = jnp.where(c % 16 == r // 16, 1.0 / 16, 0.0).astype(BF16)
    low_v = jnp.where(c % 16 == r // 16 + 8, 1.0 / 16, 0.0).astype(BF16)
    for copy in home:
        copy.wait_recv()
    bases = (acc[0:128, :], acc_core[...], acc_mate[0:128, :].astype(F32), acc_mate[128:256, :].astype(F32))
    for j, base in enumerate(bases):
        total = base + dot(mix, zin[j])
        grad_k[:, cols(j)] = (total[:, 0:QUARTER] + dot(low_k, zin4[j])).astype(BF16)
        grad_v[:, cols(j)] = (total[:, QUARTER:LANES] + dot(low_v, zin4[j])).astype(BF16)
    for copy in started:
        copy.wait_send()


COPIES = 96


def store(*refs):
    sems = refs[8]
    copies = [pltpu.make_async_copy(refs[i], refs[4 + i], sems.at[i]) for i in range(4)]
    for copy in copies:
        copy.start()
    for copy in copies:
        copy.wait()


def local(queries, key_vectors, value_vectors, slopes, w_out, grad_out):
    block = jax.ShapeDtypeStruct((B, 1024), BF16)
    vmem = pl.BlockSpec(memory_space=pltpu.VMEM)
    hbm = pl.BlockSpec(memory_space=pltpu.HBM)
    arguments = (slopes, queries, key_vectors, value_vectors, grad_out, w_out)
    results = pl.pallas_call(
        kernel,
        out_shape=[pltpu.VMEM((B, 1024), BF16)] * 4,
        in_specs=[hbm] * 6,
        out_specs=[vmem] * 4,
        scratch_shapes=[
            pltpu.SMEM((8,), F32),
            pltpu.VMEM((ROWS, LANES), BF16),
            pltpu.VMEM((384, LANES), BF16),
            pltpu.VMEM((512, QUARTER), BF16),
            pltpu.VMEM((512, QUARTER), BF16),
            pltpu.VMEM((128, 1024), BF16),
            pltpu.VMEM((128, 1024), BF16),
            pltpu.VMEM((1024, 2048), BF16),
            pltpu.VMEM((4, 32, LANES), BF16),
            pltpu.VMEM((4, 16, LANES), BF16),
            pltpu.VMEM((4, 16, QUARTER), BF16),
            pltpu.VMEM((128, QUARTER), BF16),
            pltpu.VMEM((128, LANES), BF16),
            pltpu.VMEM((64, LANES), BF16),
            pltpu.VMEM((32, LANES), BF16),
            pltpu.VMEM((HEADS, KEYS, 512), F32),
            pltpu.VMEM((HEADS, KEYS, 512), F32),
            pltpu.VMEM((HEADS, KEYS, 512), BF16),
            pltpu.VMEM((HEADS, KEYS, 512), BF16),
            pltpu.VMEM((640, LANES), BF16),
            pltpu.VMEM((128, LANES), F32),
            pltpu.VMEM((2, 192, LANES), BF16),
            pltpu.VMEM((8, 16, QUARTER), BF16),
            pltpu.VMEM((4, 64, LANES), BF16),
            pltpu.VMEM((4, 32, QUARTER), BF16),
            pltpu.VMEM((512, LANES), F32),
            pltpu.VMEM((128, LANES), F32),
            pltpu.VMEM((256, LANES), BF16),
            pltpu.VMEM((256, LANES), BF16),
            pltpu.VMEM((512, QUARTER), BF16),
            pltpu.VMEM((128, 1024), BF16),
            pltpu.VMEM((128, 1024), BF16),
            pltpu.VMEM((128, 1024), BF16),
            pltpu.VMEM((128, 1024), BF16),
            pltpu.VMEM((512, QUARTER), BF16),
            pltpu.SemaphoreType.DMA((COPIES,)),
            pltpu.SemaphoreType.DMA((COPIES,)),
            pltpu.SemaphoreType.DMA((12,)),
        ],
        compiler_params=pltpu.CompilerParams(
            collective_id=0, has_side_effects=True, vmem_limit_bytes=48 * 1024 * 1024
        ),
        cost_estimate=pl.CostEstimate(flops=2_700_000_000, bytes_accessed=8_000_000, transcendentals=1_000_000),
    )(*(pltpu.with_memory_space_constraint(x, pltpu.HBM) for x in arguments))
    return pl.pallas_call(
        store,
        out_shape=[block] * 4,
        in_specs=[vmem] * 4,
        out_specs=[hbm] * 4,
        scratch_shapes=[pltpu.SemaphoreType.DMA((4,))],
    )(*(pltpu.with_memory_space_constraint(x, pltpu.VMEM) for x in results))


def solution(mesh):
    cut = P("ctx", "head")
    return jax.shard_map(
        local,
        mesh=mesh,
        in_specs=(cut, cut, cut, P("head"), P("head", None), cut),
        out_specs=(cut, cut, cut, cut),
        check_vma=False,
    )
```

time: 63.5 us -> 56.2 us (0.89)
  Pallas kernels: 62.8 us -> 55.4 us
    pallas_call x1, Pallas kernels: 60.6 us -> 54.4 us  [local(): pl.pallas_call(kernel, out_shape=[pltpu.VMEM((B, 1024), BF16)] * 4, in_sp...]
    pallas_call x1, Pallas kernels: 2.18 us -> 1 us  [local(): pl.pallas_call(store, out_shape=[block] * 4, in_specs=[vmem] * 4, out_spe...]
where the time goes in v3:
time: 56.2 us; the launch traced here: 56.1 us
  Pallas kernels  55.4 us (99%)
  between operations  0.64 us (1%)
    pallas_call x1, Pallas kernels, local(): pl.pallas_call(kernel, out_shape=[pltpu.VMEM((B, 1024), BF16)] * 4, in_sp...  54.4 us

profile of v3, /device:TPU:1, one launch (start us, length us, event | category | flops | bytes accessed | tf_op | source)
XLA Modules:
  0.0 56.1 jit_solution(15701157540409039619)
XLA Ops:
  0.6 54.4 %shard_map.93 = (bf16[128,1024]{1,0:T(8,128)(2,1)S(1)}, bf16[128,1024]{1,0:T(8,128)(2,1)S(1)}, bf16[128,1024]{1,0:T(8,128)(2,1)S(1)}, bf16[128,1024]{1,0:T(8,128)(2,1)S(1)}) custom-call(f32[8]{0:T(128)} %slopes_in.1, bf16[128,1024]{1,0:T(8,128)(2,1)} %q.1, bf16[128,1024]{1,0:T(8,128)(2,1)} %k.1, bf16[128,1024]{1,0:T(8,128)(2,1)} %v.1, bf16[128,1024]{1,0:T(8,128)(2,1)} %g.1, ...), custom_call_target="tpu_custom_call" | custom-call | flops 2700000000 | bytes 8000000 | tf_op jit(solution)/shard_map/pallas_call | solution.py:456
  55.1 1.0 %shard_map.94 = (bf16[128,1024]{1,0:T(8,128)(2,1)}, bf16[128,1024]{1,0:T(8,128)(2,1)}, bf16[128,1024]{1,0:T(8,128)(2,1)}, bf16[128,1024]{1,0:T(8,128)(2,1)}) custom-call(bf16[128,1024]{1,0:T(8,128)(2,1)S(1)} %get-tuple-element.8.refs_0_, bf16[128,1024]{1,0:T(8,128)(2,1)S(1)} %get-tuple-element.9.refs_1_, bf16[128,1024]{1,0:T(8,128)(2,1)S(1)} %get-tuple-element.10.refs_2_, ...), custom_call_target="tpu_custom_call" | custom-call | tf_op jit(solution)/shard_map/pallas_call | solution.py:506

commit v4 on v3

v4 whole, which is shorter than its diff:
```python
import functools
import math

import jax
import jax.numpy as jnp
from jax import lax
from jax.experimental import pallas as pl
from jax.experimental.pallas import tpu as pltpu
from jax.sharding import PartitionSpec as P

B = 128
HEAD = 128
HEADS = 2
QUARTER = 256
LANES = 512
LOG_TWO = math.log(2.0)
LOG2E = 1.0 / LOG_TWO
ROOT = 1.0 / math.sqrt(HEAD)
F32 = jnp.float32
BF16 = jnp.bfloat16
MESH = pl.DeviceIdType.MESH

L1, OWN1, L2, L3, L4, L5, L6, ROWS = 0, 128, 256, 384, 512, 640, 768, 896
S1, S2, S3, S4, S5, S6, KEYS = 0, 128, 256, 384, 512, 640, 768


def flip(index, bits):
    out = index
    for bit in bits:
        side = (index // (1 << bit)) % 2
        out = out + (1 - 2 * side) * (1 << bit)
    return out


def bits_of(mask, first):
    return [first + i for i in range(3) if mask >> i & 1]


def dot(a, b, dims=((1,), (0,))):
    return lax.dot_general(a, b, (dims, ((), ())), preferred_element_type=F32)


def grid_of(rows, columns):
    r = lax.broadcasted_iota(jnp.int32, (rows, columns), 0)
    c = lax.broadcasted_iota(jnp.int32, (rows, columns), 1)
    return r, c


def pools(rows, ratios):
    blocks = []
    for ratio in ratios:
        r, c = grid_of(rows // ratio, rows)
        blocks.append(jnp.where(c // ratio == r, 1.0 / ratio, 0.0).astype(BF16))
    return jnp.concatenate(blocks, axis=0)


def spread(rows, parts):
    blocks = []
    for ratio, width, copies in parts:
        r, c = grid_of(rows, width * copies)
        blocks.append(jnp.where(r // ratio == c % width, 1.0 / ratio, 0.0).astype(BF16))
    return jnp.concatenate(blocks, axis=1)


def in_eights(x):
    return x.reshape(x.shape[0] // 8, 8, x.shape[1])


def kernel(
    slopes_in, q, k, v, g, w_in,
    layer_out, grad_q, grad_k, grad_v,
    slopes, kv, kvo, kt, qc, qm, gc, gm, gown, gfar, w, s1, s2, s3, a4, a5, a6,
    scores, gradw, prob, dsc, scores_o, gradw_o, prob_o, dsc_o, stat_out, stat_in, final_out, final_in,
    out, out123, back, zin, acc, acc_core,
    far_q, far_attn, near_q, near_attn, rest_q, rest_attn, whole, ga, send_part, recv_part,
    send_sem, recv_sem, local_sem,
):
    ctx = lax.axis_index("ctx")
    head = lax.axis_index("head")
    core = ctx % 2
    place = (ctx // 2) % 2

    def cols(j):
        a, c = j // 2, j % 2
        number = (place + a - 2 * place * a) * 2 + (core + c - 2 * core * c)
        return pl.ds(pl.multiple_of(number * QUARTER, QUARTER), QUARTER)

    my_cols = pl.ds(pl.multiple_of(head * 1024, 1024), 1024)
    far_cols = pl.ds(pl.multiple_of((1 - head) * 1024, 1024), 1024)

    across = (ctx, 1 - head)
    z_peer = [[(flip(ctx, [0] * sub + bits_of(m, 1)), head) for sub in range(2)] for m in range(8)]
    other = z_peer[0][1]
    xy_peer = [None] + [(flip(ctx, bits_of(m, 4)), head) for m in range(1, 8)]

    def load(src, dst, slot):
        copy = pltpu.make_async_copy(src, dst, local_sem.at[slot])
        copy.start()
        return copy

    load_kv = []
    for j in range(4):
        into, at = (kvo, 0) if j % 2 == 0 else (kt, 0)
        left = LANES * (j // 2)
        load_kv.append(load(k.at[:, cols(j)], into.at[0:128, left:left + QUARTER], 2 * j))
        load_kv.append(load(v.at[:, cols(j)], into.at[0:128, left + QUARTER:left + LANES], 2 * j + 1))

    barrier = pltpu.get_barrier_semaphore()
    peers = [other, across] + sum(z_peer[1:], []) + xy_peer[1:]
    for peer in peers:
        pl.semaphore_signal(barrier, inc=1, device_id=peer, device_id_type=MESH)

    load_rest = [
        load(q.at[:, cols(0)], qc.at[0:128, :], 8),
        load(q.at[:, cols(2)], qm.at[0:128, :], 9),
        load(g, gown, 10),
        load(slopes_in, slopes, 11),
    ]
    stat_out[...] = jnp.zeros_like(stat_out)
    final_out[...] = jnp.zeros_like(final_out)
    for copy in load_kv:
        copy.wait()
    load_rest.append(load(w_in, w, 12))
    means = pools(128, (2, 4, 8))
    for j in range(4):
        left = LANES * (j // 2)
        pooled = dot(means, kvo[0:128, left:left + LANES] if j % 2 == 0 else kt[:, left:left + LANES]).astype(BF16)
        s1[j] = pooled[0:64]
        s2[j] = pooled[64:96]
        s3[j] = pooled[96:112]

    pl.semaphore_wait(barrier, len(peers))

    count = [0]
    started = []

    def send(src, dst, peer):
        slot = count[0]
        count[0] += 1
        copy = pltpu.make_async_remote_copy(
            src_ref=src, dst_ref=dst, send_sem=send_sem.at[slot], recv_sem=recv_sem.at[slot],
            device_id=peer, device_id_type=MESH,
        )
        copy.start()
        started.append(copy)
        return copy

    pair_peer = [None, other, z_peer[1][0], z_peer[1][1]]

    def at_pair(ref, j):
        return ref.at[128 * j:128 * j + 128, :]

    def z_sends(source, low, rows, masks):
        return [
            send(
                source.at[2 * (m % 2) + sub],
                kv.at[low + (2 * i + sub) * rows:low + (2 * i + sub + 1) * rows, :],
                z_peer[m][sub],
            )
            for i, m in enumerate(masks)
            for sub in range(2)
        ]

    in3 = z_sends(s3, L3, 16, (4, 5, 6, 7))
    in_g = send(g, gfar, across)
    in_kv = send(kt, kvo.at[128:256, :], other)
    in_q_core = [send(q.at[:, cols(1)], at_pair(qc, 1), other), send(q.at[:, cols(3)], at_pair(qm, 1), other)]
    in2 = z_sends(s2, L2, 32, (2, 3))
    in1 = z_sends(s1, L1, 64, (1,))
    in_q = [send(q.at[:, cols(j)], at_pair(qc, j), pair_peer[j]) for j in range(2, 4)]

    in_kv.wait_recv()
    kv[OWN1:L2, :] = dot(pools(256, (2,)), kvo[:, 0:LANES]).astype(BF16)
    a4[0:16, :] = dot(pools(256, (16,)), kvo[:, 0:LANES]).astype(BF16)

    def xy_sends(half):
        copies = [send(a4.at[64 * half:64 * half + 64, :], kv.at[L4 + 64 * half:L4 + 64 * half + 64, :], xy_peer[1])]
        for m in range(2, 4):
            low = L5 + 64 * (m - 2) + 32 * half
            copies.append(send(a5.at[32 * half:32 * half + 32, :], kv.at[low:low + 32, :], xy_peer[m]))
        for m in range(4, 8):
            low = L6 + 32 * (m - 4) + 16 * half
            copies.append(send(a6.at[16 * half:16 * half + 16, :], kv.at[low:low + 16, :], xy_peer[m]))
        return copies

    for copy in in3:
        copy.wait_recv()
    upper = dot(pools(128, (2, 4, 8)), kv[L3:L4, :]).astype(BF16)
    a4[64:128, :] = upper[0:64]
    a5[32:64, :] = upper[64:96]
    a6[16:32, :] = upper[96:112]
    far = xy_sends(1)

    for copy in load_rest:
        copy.wait()
    in_g.wait_recv()
    ga[...] = (
        dot(gown[...], w[:, my_cols], ((1,), (1,))) + dot(gfar[...], w[:, far_cols], ((1,), (1,)))
    ).astype(BF16)
    in_ga = [send(ga.at[:, cols(j)], at_pair(gc, j), pair_peer[j]) for j in range(2, 4)]
    in_ga_core = [send(ga.at[:, cols(1)], at_pair(gc, 1), other), send(ga.at[:, cols(3)], at_pair(gm, 1), other)]
    gc[0:128, :] = ga[:, cols(0)]
    gm[0:128, :] = ga[:, cols(2)]

    lane = lax.broadcasted_iota(jnp.int32, (1, 256), 1)

    def level_bias(t, h, level):
        slope = slopes[((place + t - 2 * place * t) * 2 + core) * HEADS + h]
        return (level * LOG_TWO - slope * (level + 1.0)) * LOG2E

    def key_lanes(h, t=0):
        return slice(LANES * t + h * HEAD, LANES * t + (h + 1) * HEAD)

    def value_lanes(h, t=0):
        return slice(LANES * t + QUARTER + h * HEAD, LANES * t + QUARTER + (h + 1) * HEAD)

    def queries_of(chip):
        return slice(256 * chip, 256 * chip + 256)

    def head_of(h):
        return slice(h * HEAD, (h + 1) * HEAD)

    def across_lanes(x):
        return jnp.sum(x, axis=0, keepdims=True)

    def own_stats(t, h):
        by, to = (qc, gc) if t == 0 else (qm, gm)
        u = 2 * t + h
        tops = []
        for at in (0, 128):
            rows = slice(at, at + 128)
            bias = jnp.where((lane < 128) == (at == 0), 0.0, level_bias(t, h, 0))
            s = dot(kvo[rows, key_lanes(h, t)], by[0:256, head_of(h)], ((1,), (1,))) * (ROOT * LOG2E) + bias
            scores_o[u, rows, :] = s
            tops.append(jnp.max(in_eights(s), axis=0))
        top = jnp.max(jnp.maximum(tops[0], tops[1]), axis=0, keepdims=True)
        total = jnp.zeros((8, 256), F32)
        center = jnp.zeros((8, 256), F32)
        for at in (0, 128):
            rows = slice(at, at + 128)
            e = jnp.exp2(scores_o[u, rows, :] - top)
            scores_o[u, rows, :] = e
            toward = dot(kvo[rows, value_lanes(h, t)], to[0:256, head_of(h)], ((1,), (1,)))
            gradw_o[u, rows, :] = toward
            total = total + jnp.sum(in_eights(e), axis=0)
            center = center + jnp.sum(in_eights(e * toward), axis=0)
        return top, across_lanes(total), across_lanes(center)

    for copy in in_q_core + in_ga_core:
        copy.wait_recv()
    for h in range(HEADS):
        for n, stat in enumerate(own_stats(1, h)):
            stat_out[3 * h + n:3 * h + n + 1, :] = stat
    in_stat = send(stat_out, stat_in, z_peer[1][0])
    near_stats = [own_stats(0, h) for h in range(HEADS)]

    for copy in in1 + in2:
        copy.wait_recv()
    a4[16:32, :] = dot(pools(128, (8,)), kv[L1:L1 + 128, :]).astype(BF16)
    a4[32:64, :] = dot(pools(128, (4,)), kv[L2:L3, :]).astype(BF16)
    upper = dot(pools(64, (2, 4)), a4[0:64, :]).astype(BF16)
    a5[0:32, :] = upper[0:32]
    a6[0:16, :] = upper[32:48]
    far += xy_sends(0)

    def key_row(chip, at):
        return L1 + 128 * chip if at == S1 else L2 + at - S2

    def exponents(unit, places):
        h, chip = unit
        own = queries_of(chip)
        tops = []
        for at in places:
            row = key_row(chip, at)
            s = dot(kv[row:row + 128, key_lanes(h)], qc[own, head_of(h)], ((1,), (1,))) * (ROOT * LOG2E)
            s = s + level_bias(0, h, at // 128 + 1)
            scores[h, at:at + 128, own] = s
            tops.append(jnp.max(in_eights(s), axis=0))
        top = jnp.max(functools.reduce(jnp.maximum, tops), axis=0, keepdims=True)
        total = jnp.zeros((8, 256), F32)
        for at in places:
            e = jnp.exp2(scores[h, at:at + 128, own] - top)
            scores[h, at:at + 128, own] = e
            total = total + jnp.sum(in_eights(e), axis=0)
        return top, across_lanes(total)

    def toward_center(unit, places):
        h, chip = unit
        own = queries_of(chip)
        center = jnp.zeros((8, 256), F32)
        for at in places:
            row = key_row(chip, at)
            toward = dot(kv[row:row + 128, value_lanes(h)], gc[own, head_of(h)], ((1,), (1,)))
            gradw[h, at:at + 128, own] = toward
            center = center + jnp.sum(in_eights(scores[h, at:at + 128, own] * toward), axis=0)
        return across_lanes(center)

    units = [(h, chip) for chip in range(2) for h in range(HEADS)]
    parts = ((S1, S2, S3), (S4, S5, S6))
    tops = {unit: [] for unit in units}
    totals = {unit: [] for unit in units}
    sums = {unit: [] for unit in units}

    def add_exponents(unit, places):
        top, total = exponents(unit, places)
        tops[unit].append(top)
        totals[unit].append(total)

    for unit in units[0:2]:
        add_exponents(unit, parts[0])
        sums[unit].append(toward_center(unit, parts[0]))
    for copy in in_q:
        copy.wait_recv()
    for unit in units[2:4]:
        add_exponents(unit, parts[0])
    for copy in far:
        copy.wait_recv()
    for unit in units[0:2]:
        add_exponents(unit, parts[1])
        sums[unit].append(toward_center(unit, parts[1]))
    for unit in units[2:4]:
        add_exponents(unit, parts[1])
    in_stat.wait_recv()
    for copy in in_ga:
        copy.wait_recv()
    for unit in units[2:4]:
        for places in parts:
            sums[unit].append(toward_center(unit, places))

    scales, centers = {}, {}
    for unit in units:
        h, chip = unit
        if chip == 0:
            stat = near_stats[h]
        else:
            stat = tuple(stat_in[3 * h + n:3 * h + n + 1, :] for n in range(3))
        every = tops[unit] + [stat[0]]
        best = functools.reduce(jnp.maximum, every)
        factors = [jnp.exp2(top - best) for top in every]
        inverse = 1.0 / sum(f * total for f, total in zip(factors, totals[unit] + [stat[1]]))
        centers[unit] = sum(f * part for f, part in zip(factors, sums[unit] + [stat[2]])) * inverse
        scales[unit] = [f * inverse for f in factors]
        if chip == 1:
            final_out[2 * h:2 * h + 1, :] = scales[unit][2]
            final_out[2 * h + 1:2 * h + 2, :] = centers[unit]
    in_final = send(final_out, final_in, z_peer[1][0])

    def normalise(h, n):
        for chip in range(2):
            own = queries_of(chip)
            for at in parts[n]:
                weight = scores[h, at:at + 128, own] * scales[h, chip][n]
                prob[h, at:at + 128, own] = weight.astype(BF16)
                dsc[h, at:at + 128, own] = (weight * (gradw[h, at:at + 128, own] - centers[h, chip])).astype(BF16)

    def gradients(h, low, high, own=slice(0, 512)):
        d_key = dot(dsc[h, low:high, own], qc[own, head_of(h)]) * ROOT
        d_value = dot(prob[h, low:high, own], gc[own, head_of(h)])
        return d_key, d_value

    def piece(low, rows):
        return out.at[low:low + rows, :]

    for h in range(HEADS):
        normalise(h, 1)
        d_key, d_value = gradients(h, S4, KEYS)
        out[S4:KEYS, key_lanes(h)] = d_key.astype(BF16)
        out[S4:KEYS, value_lanes(h)] = d_value.astype(BF16)

    def xy_back(half):
        copies = [send(piece(S4 + 64 * half, 64), back.at[half, 0:64, :], xy_peer[1])]
        for m in range(2, 4):
            at = 64 + 32 * (m - 2)
            copies.append(send(piece(S5 + 64 * (m - 2) + 32 * half, 32), back.at[half, at:at + 32, :], xy_peer[m]))
        for m in range(4, 8):
            at = 128 + 16 * (m - 4)
            copies.append(send(piece(S6 + 32 * (m - 4) + 16 * half, 16), back.at[half, at:at + 16, :], xy_peer[m]))
        return copies

    back_near = xy_back(0)
    back_far = xy_back(1)

    for h in range(HEADS):
        normalise(h, 0)

    def to_queries(h, chip, lanes, weights):
        own, level1 = queries_of(chip), key_row(chip, S1)
        total = dot(kv[L2:ROWS, lanes], weights[h, S2:KEYS, own], ((0,), (0,)))
        return (total + dot(kv[level1:level1 + 128, lanes], weights[h, S1:S2, own], ((0,), (0,)))).T

    for h in range(HEADS):
        far_attn[:, head_of(h)] = to_queries(h, 1, value_lanes(h), prob).astype(BF16)
    in_rest_attn = [send(at_pair(far_attn, i), rest_attn.at[i], pair_peer[2 + i]) for i in range(2)]
    for h in range(HEADS):
        far_q[:, head_of(h)] = (to_queries(h, 1, key_lanes(h), dsc) * ROOT).astype(BF16)
    in_rest_q = [send(at_pair(far_q, i), rest_q.at[i], pair_peer[2 + i]) for i in range(2)]

    for h in range(HEADS):
        d_key, d_value = gradients(h, S2, S4)
        out123[128:384, key_lanes(h)] = d_key
        out123[128:384, value_lanes(h)] = d_value
        d_key, d_value = gradients(h, S1, S2, queries_of(0))
        out123[0:128, key_lanes(h)] = d_key
        out123[0:128, value_lanes(h)] = d_value

    double = spread(256, ((2, 128, 1),))
    in_near = []
    for t in range(2):
        if t == 1:
            in_final.wait_recv()
        by, to = (qc, gc) if t == 0 else (qm, gm)
        for h in range(HEADS):
            u = 2 * t + h
            if t == 0:
                scale, center = scales[h, 0][2], centers[h, 0]
            else:
                scale, center = final_in[2 * h:2 * h + 1, :], final_in[2 * h + 1:2 * h + 2, :]
            weight = scores_o[u] * scale
            prob_o[u] = weight.astype(BF16)
            dsc_o[u] = (weight * (gradw_o[u] - center)).astype(BF16)
            for weights, source, beyond, lanes, factor in (
                (dsc_o, by, dsc, key_lanes(h, t), ROOT), (prob_o, to, prob, value_lanes(h, t), 1.0)
            ):
                total = dot(weights[u], source[0:256, head_of(h)])
                if t == 0:
                    level1 = dot(double, beyond[h, S1:S2, 256:512]).astype(BF16)
                    total = total + dot(level1, source[256:512, head_of(h)])
                acc[:, lanes] = total * factor
            attn_part = dot(kvo[:, value_lanes(h, t)], prob_o[u], ((0,), (0,))).T
            q_part = dot(kvo[:, key_lanes(h, t)], dsc_o[u], ((0,), (0,))).T
            if t == 0:
                attn_part = attn_part + to_queries(h, 0, value_lanes(h), prob)
                q_part = q_part + to_queries(h, 0, key_lanes(h), dsc)
            near_attn[t, :, head_of(h)] = attn_part.astype(BF16)
            near_q[t, :, head_of(h)] = (q_part * ROOT).astype(BF16)
        if t == 0:
            in_near += [send(near_attn.at[0, 128:256, :], whole.at[:, cols(0)], other)]
            in_near += [send(near_q.at[0, 128:256, :], grad_q.at[:, cols(0)], other)]
        else:
            in_near += [send(near_attn.at[1, 128:256, :], rest_attn.at[2], other)]
            in_near += [send(near_q.at[1, 128:256, :], rest_q.at[2], other)]

    for copy in back_near:
        copy.wait_recv()
    g4 = dot(spread(64, ((1, 64, 1), (2, 32, 2), (4, 16, 4))), back[0]).astype(BF16)
    out[0:128, :] = (out123[0:128, :] + dot(spread(128, ((8, 16, 1),)), g4[16:32])).astype(BF16)
    out[128:256, :] = (out123[128:256, :] + dot(spread(128, ((4, 32, 1),)), g4[32:64])).astype(BF16)
    home = [send(piece(S1 + 64 * sub, 64), zin.at[2 + sub, 0:64, :], z_peer[1][sub]) for sub in range(2)]
    home += [
        send(piece(S2 + (2 * i + sub) * 32, 32), zin.at[2 * (m % 2) + sub, 64:96, :], z_peer[m][sub])
        for i, m in enumerate((2, 3))
        for sub in range(2)
    ]
    acc[:, 0:LANES] += dot(spread(256, ((16, 16, 1),)), g4[0:16])
    home += [send(acc.at[128:256, :], acc_core, other)]

    for copy in back_far:
        copy.wait_recv()
    mix = spread(128, ((2, 64, 1), (4, 32, 2), (8, 16, 4)))
    out[S3:S4, :] = (out123[256:384, :] + dot(mix, back[1])).astype(BF16)
    home += [
        send(
            piece(S3 + (2 * i + sub) * 16, 16),
            zin.at[2 * (m % 2) + sub, 96 + 16 * (i // 2):112 + 16 * (i // 2), :],
            z_peer[m][sub],
        )
        for i, m in enumerate((4, 5, 6, 7))
        for sub in range(2)
    ]

    whole[:, cols(0)] = near_attn[0, 0:128, :]
    grad_q[:, cols(0)] = near_q[0, 0:128, :]
    for copy in in_near + in_rest_attn:
        copy.wait_recv()
    whole[:, cols(2)] = (near_attn[1, 0:128, :].astype(F32) + rest_attn[0].astype(F32)).astype(BF16)
    whole[:, cols(3)] = (rest_attn[2].astype(F32) + rest_attn[1].astype(F32)).astype(BF16)
    send_part[...] = dot(whole[...], w[:, far_cols]).astype(BF16)
    part = send(send_part, recv_part, across)
    for copy in in_rest_q:
        copy.wait_recv()
    grad_q[:, cols(2)] = (near_q[1, 0:128, :].astype(F32) + rest_q[0].astype(F32)).astype(BF16)
    grad_q[:, cols(3)] = (rest_q[2].astype(F32) + rest_q[1].astype(F32)).astype(BF16)
    own_part = dot(whole[...], w[:, my_cols])
    part.wait_recv()
    layer_out[...] = (own_part + recv_part[...].astype(F32)).astype(BF16)

    mix = spread(128, ((2, 64, 1), (4, 32, 1), (8, 16, 2)))
    for copy in home:
        copy.wait_recv()
    bases = (acc[0:128, 0:LANES], acc_core[:, 0:LANES], acc[0:128, LANES:1024], acc_core[:, LANES:1024])
    for j, base in enumerate(bases):
        low = 64 if j < 2 else 0
        total = (base + dot(mix[:, low:128], zin[j, low:128, :])).astype(BF16)
        grad_k[:, cols(j)] = total[:, 0:QUARTER]
        grad_v[:, cols(j)] = total[:, QUARTER:LANES]
    for copy in started:
        copy.wait_send()


COPIES = 96


def store(*refs):
    sems = refs[8]
    copies = [pltpu.make_async_copy(refs[i], refs[4 + i], sems.at[i]) for i in range(4)]
    for copy in copies:
        copy.start()
    for copy in copies:
        copy.wait()


def local(queries, key_vectors, value_vectors, slopes, w_out, grad_out):
    block = jax.ShapeDtypeStruct((B, 1024), BF16)
    vmem = pl.BlockSpec(memory_space=pltpu.VMEM)
    hbm = pl.BlockSpec(memory_space=pltpu.HBM)
    arguments = (slopes, queries, key_vectors, value_vectors, grad_out, w_out)
    results = pl.pallas_call(
        kernel,
        out_shape=[pltpu.VMEM((B, 1024), BF16)] * 4,
        in_specs=[hbm] * 6,
        out_specs=[vmem] * 4,
        scratch_shapes=[
            pltpu.SMEM((8,), F32),
            pltpu.VMEM((ROWS, LANES), BF16),
            pltpu.VMEM((256, 1024), BF16),
            pltpu.VMEM((128, 1024), BF16),
            pltpu.VMEM((512, QUARTER), BF16),
            pltpu.VMEM((256, QUARTER), BF16),
            pltpu.VMEM((512, QUARTER), BF16),
            pltpu.VMEM((256, QUARTER), BF16),
            pltpu.VMEM((128, 1024), BF16),
            pltpu.VMEM((128, 1024), BF16),
            pltpu.VMEM((1024, 2048), BF16),
            pltpu.VMEM((4, 64, LANES), BF16),
            pltpu.VMEM((4, 32, LANES), BF16),
            pltpu.VMEM((4, 16, LANES), BF16),
            pltpu.VMEM((128, LANES), BF16),
            pltpu.VMEM((64, LANES), BF16),
            pltpu.VMEM((32, LANES), BF16),
            pltpu.VMEM((HEADS, KEYS, 512), F32),
            pltpu.VMEM((HEADS, KEYS, 512), F32),
            pltpu.VMEM((HEADS, KEYS, 512), BF16),
            pltpu.VMEM((HEADS, KEYS, 512), BF16),
            pltpu.VMEM((4, 256, 256), F32),
            pltpu.VMEM((4, 256, 256), F32),
            pltpu.VMEM((4, 256, 256), BF16),
            pltpu.VMEM((4, 256, 256), BF16),
            pltpu.VMEM((8, 256), F32),
            pltpu.VMEM((8, 256), F32),
            pltpu.VMEM((8, 256), F32),
            pltpu.VMEM((8, 256), F32),
            pltpu.VMEM((KEYS, LANES), BF16),
            pltpu.VMEM((384, LANES), F32),
            pltpu.VMEM((2, 192, LANES), BF16),
            pltpu.VMEM((4, 128, LANES), BF16),
            pltpu.VMEM((256, 1024), F32),
            pltpu.VMEM((128, 1024), F32),
            pltpu.VMEM((256, QUARTER), BF16),
            pltpu.VMEM((256, QUARTER), BF16),
            pltpu.VMEM((2, 256, QUARTER), BF16),
            pltpu.VMEM((2, 256, QUARTER), BF16),
            pltpu.VMEM((3, 128, QUARTER), BF16),
            pltpu.VMEM((3, 128, QUARTER), BF16),
            pltpu.VMEM((128, 1024), BF16),
            pltpu.VMEM((128, 1024), BF16),
            pltpu.VMEM((128, 1024), BF16),
            pltpu.VMEM((128, 1024), BF16),
            pltpu.SemaphoreType.DMA((COPIES,)),
            pltpu.SemaphoreType.DMA((COPIES,)),
            pltpu.SemaphoreType.DMA((13,)),
        ],
        compiler_params=pltpu.CompilerParams(
            collective_id=0, has_side_effects=True, vmem_limit_bytes=48 * 1024 * 1024
        ),
        cost_estimate=pl.CostEstimate(flops=2_700_000_000, bytes_accessed=8_000_000, transcendentals=1_000_000),
    )(*(pltpu.with_memory_space_constraint(x, pltpu.HBM) for x in arguments))
    return pl.pallas_call(
        store,
        out_shape=[block] * 4,
        in_specs=[vmem] * 4,
        out_specs=[hbm] * 4,
        scratch_shapes=[pltpu.SemaphoreType.DMA((4,))],
    )(*(pltpu.with_memory_space_constraint(x, pltpu.VMEM) for x in results))


def solution(mesh):
    cut = P("ctx", "head")
    return jax.shard_map(
        local,
        mesh=mesh,
        in_specs=(cut, cut, cut, P("head"), P("head", None), cut),
        out_specs=(cut, cut, cut, cut),
        check_vma=False,
    )
```

time: 56.2 us -> 51.4 us (0.915)
  Pallas kernels: 55.4 us -> 50.6 us
    pallas_call x1, Pallas kernels: 54.4 us -> 49.6 us  [local(): pl.pallas_call(kernel, out_shape=[pltpu.VMEM((B, 1024), BF16)] * 4, in_sp...]
where the time goes in v4:
time: 51.4 us; the launch traced here: 51.3 us
  Pallas kernels  50.6 us (98%)
  between operations  0.64 us (1%)
    pallas_call x1, Pallas kernels, local(): pl.pallas_call(kernel, out_shape=[pltpu.VMEM((B, 1024), BF16)] * 4, in_sp...  49.6 us

profile of v4, /device:TPU:1, one launch (start us, length us, event | category | flops | bytes accessed | tf_op | source)
XLA Modules:
  0.0 51.3 jit_solution(10551812093403534515)
XLA Ops:
  0.6 49.6 %shard_map.93 = (bf16[128,1024]{1,0:T(8,128)(2,1)S(1)}, bf16[128,1024]{1,0:T(8,128)(2,1)S(1)}, bf16[128,1024]{1,0:T(8,128)(2,1)S(1)}, bf16[128,1024]{1,0:T(8,128)(2,1)S(1)}) custom-call(f32[8]{0:T(128)} %slopes_in.1, bf16[128,1024]{1,0:T(8,128)(2,1)} %q.1, bf16[128,1024]{1,0:T(8,128)(2,1)} %k.1, bf16[128,1024]{1,0:T(8,128)(2,1)} %v.1, bf16[128,1024]{1,0:T(8,128)(2,1)} %g.1, ...), custom_call_target="tpu_custom_call" | custom-call | flops 2700000000 | bytes 8000000 | tf_op jit(solution)/shard_map/pallas_call | solution.py:517
  50.3 1.0 %shard_map.94 = (bf16[128,1024]{1,0:T(8,128)(2,1)}, bf16[128,1024]{1,0:T(8,128)(2,1)}, bf16[128,1024]{1,0:T(8,128)(2,1)}, bf16[128,1024]{1,0:T(8,128)(2,1)}) custom-call(bf16[128,1024]{1,0:T(8,128)(2,1)S(1)} %get-tuple-element.8.refs_0_, bf16[128,1024]{1,0:T(8,128)(2,1)S(1)} %get-tuple-element.9.refs_1_, bf16[128,1024]{1,0:T(8,128)(2,1)S(1)} %get-tuple-element.10.refs_2_, ...), custom_call_target="tpu_custom_call" | custom-call | tf_op jit(solution)/shard_map/pallas_call | solution.py:577

commit v5 on v4

--- a/solution.py
+++ b/solution.py
@@ -69,7 +69,7 @@
 def kernel(
     slopes_in, q, k, v, g, w_in,
     layer_out, grad_q, grad_k, grad_v,
-    slopes, kv, kvo, kt, qc, qm, gc, gm, gown, gfar, w, s1, s2, s3, a4, a5, a6,
+    slopes, kv, kvo, kt, qc, qm, gc, gm, gown, gfar, w, s1, s2, s3, mate3, a4, a5, a6,
     scores, gradw, prob, dsc, scores_o, gradw_o, prob_o, dsc_o, stat_out, stat_in, final_out, final_in,
     out, out123, back, zin, acc, acc_core,
     far_q, far_attn, near_q, near_attn, rest_q, rest_attn, whole, ga, send_part, recv_part,
@@ -162,11 +162,12 @@
         ]
 
     in3 = z_sends(s3, L3, 16, (4, 5, 6, 7))
-    in_g = send(g, gfar, across)
-    in_kv = send(kt, kvo.at[128:256, :], other)
-    in_q_core = [send(q.at[:, cols(1)], at_pair(qc, 1), other), send(q.at[:, cols(3)], at_pair(qm, 1), other)]
+    in_mate = [send(s3.at[2 + sub], mate3.at[16 * sub:16 * sub + 16, :], z_peer[1][sub]) for sub in range(2)]
     in2 = z_sends(s2, L2, 32, (2, 3))
     in1 = z_sends(s1, L1, 64, (1,))
+    in_kv = send(kt, kvo.at[128:256, :], other)
+    in_g = send(g, gfar, across)
+    in_q_core = [send(q.at[:, cols(1)], at_pair(qc, 1), other), send(q.at[:, cols(3)], at_pair(qm, 1), other)]
     in_q = [send(q.at[:, cols(j)], at_pair(qc, j), pair_peer[j]) for j in range(2, 4)]
 
     in_kv.wait_recv()
@@ -246,22 +247,23 @@
             center = center + jnp.sum(in_eights(e * toward), axis=0)
         return top, across_lanes(total), across_lanes(center)
 
-    for copy in in_q_core + in_ga_core:
-        copy.wait_recv()
-    for h in range(HEADS):
-        for n, stat in enumerate(own_stats(1, h)):
-            stat_out[3 * h + n:3 * h + n + 1, :] = stat
-    in_stat = send(stat_out, stat_in, z_peer[1][0])
-    near_stats = [own_stats(0, h) for h in range(HEADS)]
-
-    for copy in in1 + in2:
-        copy.wait_recv()
-    a4[16:32, :] = dot(pools(128, (8,)), kv[L1:L1 + 128, :]).astype(BF16)
+    for copy in in_mate + in2:
+        copy.wait_recv()
+    a4[16:32, :] = dot(pools(32, (2,)), mate3[...]).astype(BF16)
     a4[32:64, :] = dot(pools(128, (4,)), kv[L2:L3, :]).astype(BF16)
     upper = dot(pools(64, (2, 4)), a4[0:64, :]).astype(BF16)
     a5[0:32, :] = upper[0:32]
     a6[0:16, :] = upper[32:48]
     far += xy_sends(0)
+
+    for copy in in_q_core + in_ga_core:
+        copy.wait_recv()
+    near_stats = [own_stats(0, h) for h in range(HEADS)]
+
+    for h in range(HEADS):
+        for n, stat in enumerate(own_stats(1, h)):
+            stat_out[3 * h + n:3 * h + n + 1, :] = stat
+    in_stat = send(stat_out, stat_in, z_peer[1][0])
 
     def key_row(chip, at):
         return L1 + 128 * chip if at == S1 else L2 + at - S2
@@ -296,36 +298,39 @@
         return across_lanes(center)
 
     units = [(h, chip) for chip in range(2) for h in range(HEADS)]
-    parts = ((S1, S2, S3), (S4, S5, S6))
-    tops = {unit: [] for unit in units}
-    totals = {unit: [] for unit in units}
-    sums = {unit: [] for unit in units}
-
-    def add_exponents(unit, places):
-        top, total = exponents(unit, places)
-        tops[unit].append(top)
-        totals[unit].append(total)
+    parts = ((S2, S3), (S4, S5, S6), (S1,))
+    tops, totals, sums = ({unit: {} for unit in units} for _ in range(3))
+
+    def add_exponents(unit, n):
+        tops[unit][n], totals[unit][n] = exponents(unit, parts[n])
+
+    def add_center(unit, n):
+        sums[unit][n] = toward_center(unit, parts[n])
 
     for unit in units[0:2]:
-        add_exponents(unit, parts[0])
-        sums[unit].append(toward_center(unit, parts[0]))
+        add_exponents(unit, 0)
+        add_center(unit, 0)
     for copy in in_q:
         copy.wait_recv()
     for unit in units[2:4]:
-        add_exponents(unit, parts[0])
-    for copy in far:
-        copy.wait_recv()
-    for unit in units[0:2]:
-        add_exponents(unit, parts[1])
-        sums[unit].append(toward_center(unit, parts[1]))
-    for unit in units[2:4]:
-        add_exponents(unit, parts[1])
+        add_exponents(unit, 0)
+        add_exponents(unit, 2)
     in_stat.wait_recv()
     for copy in in_ga:
         copy.wait_recv()
     for unit in units[2:4]:
-        for places in parts:
-            sums[unit].append(toward_center(unit, places))
+        add_center(unit, 0)
+        add_center(unit, 2)
+    for copy in far:
+        copy.wait_recv()
+    for unit in units[2:4] + units[0:2]:
+        add_exponents(unit, 1)
+        add_center(unit, 1)
+    for copy in in1:
+        copy.wait_recv()
+    for unit in units[0:2]:
+        add_exponents(unit, 2)
+        add_center(unit, 2)
 
     scales, centers = {}, {}
     for unit in units:
@@ -334,24 +339,25 @@
             stat = near_stats[h]
         else:
             stat = tuple(stat_in[3 * h + n:3 * h + n + 1, :] for n in range(3))
-        every = tops[unit] + [stat[0]]
+        every = [tops[unit][n] for n in range(3)] + [stat[0]]
+        masses = [totals[unit][n] for n in range(3)] + [stat[1]]
+        weighted = [sums[unit][n] for n in range(3)] + [stat[2]]
         best = functools.reduce(jnp.maximum, every)
         factors = [jnp.exp2(top - best) for top in every]
-        inverse = 1.0 / sum(f * total for f, total in zip(factors, totals[unit] + [stat[1]]))
-        centers[unit] = sum(f * part for f, part in zip(factors, sums[unit] + [stat[2]])) * inverse
+        inverse = 1.0 / sum(f * mass for f, mass in zip(factors, masses))
+        centers[unit] = sum(f * part for f, part in zip(factors, weighted)) * inverse
         scales[unit] = [f * inverse for f in factors]
         if chip == 1:
-            final_out[2 * h:2 * h + 1, :] = scales[unit][2]
+            final_out[2 * h:2 * h + 1, :] = scales[unit][3]
             final_out[2 * h + 1:2 * h + 2, :] = centers[unit]
     in_final = send(final_out, final_in, z_peer[1][0])
 
-    def normalise(h, n):
-        for chip in range(2):
-            own = queries_of(chip)
-            for at in parts[n]:
-                weight = scores[h, at:at + 128, own] * scales[h, chip][n]
-                prob[h, at:at + 128, own] = weight.astype(BF16)
-                dsc[h, at:at + 128, own] = (weight * (gradw[h, at:at + 128, own] - centers[h, chip])).astype(BF16)
+    def normalise(h, chip, n):
+        own = queries_of(chip)
+        for at in parts[n]:
+            weight = scores[h, at:at + 128, own] * scales[h, chip][n]
+            prob[h, at:at + 128, own] = weight.astype(BF16)
+            dsc[h, at:at + 128, own] = (weight * (gradw[h, at:at + 128, own] - centers[h, chip])).astype(BF16)
 
     def gradients(h, low, high, own=slice(0, 512)):
         d_key = dot(dsc[h, low:high, own], qc[own, head_of(h)]) * ROOT
@@ -361,8 +367,22 @@
     def piece(low, rows):
         return out.at[low:low + rows, :]
 
+    def to_queries(h, chip, lanes, weights):
+        own, level1 = queries_of(chip), key_row(chip, S1)
+        total = dot(kv[L2:ROWS, lanes], weights[h, S2:KEYS, own], ((0,), (0,)))
+        return (total + dot(kv[level1:level1 + 128, lanes], weights[h, S1:S2, own], ((0,), (0,)))).T
+
     for h in range(HEADS):
-        normalise(h, 1)
+        for n in range(3):
+            normalise(h, 1, n)
+        far_attn[:, head_of(h)] = to_queries(h, 1, value_lanes(h), prob).astype(BF16)
+    in_rest_attn = [send(at_pair(far_attn, i), rest_attn.at[i], pair_peer[2 + i]) for i in range(2)]
+    for h in range(HEADS):
+        far_q[:, head_of(h)] = (to_queries(h, 1, key_lanes(h), dsc) * ROOT).astype(BF16)
+    in_rest_q = [send(at_pair(far_q, i), rest_q.at[i], pair_peer[2 + i]) for i in range(2)]
+
+    for h in range(HEADS):
+        normalise(h, 0, 1)
         d_key, d_value = gradients(h, S4, KEYS)
         out[S4:KEYS, key_lanes(h)] = d_key.astype(BF16)
         out[S4:KEYS, value_lanes(h)] = d_value.astype(BF16)
@@ -381,20 +401,8 @@
     back_far = xy_back(1)
 
     for h in range(HEADS):
-        normalise(h, 0)
-
-    def to_queries(h, chip, lanes, weights):
-        own, level1 = queries_of(chip), key_row(chip, S1)
-        total = dot(kv[L2:ROWS, lanes], weights[h, S2:KEYS, own], ((0,), (0,)))
-        return (total + dot(kv[level1:level1 + 128, lanes], weights[h, S1:S2, own], ((0,), (0,)))).T
-
-    for h in range(HEADS):
-        far_attn[:, head_of(h)] = to_queries(h, 1, value_lanes(h), prob).astype(BF16)
-    in_rest_attn = [send(at_pair(far_attn, i), rest_attn.at[i], pair_peer[2 + i]) for i in range(2)]
-    for h in range(HEADS):
-        far_q[:, head_of(h)] = (to_queries(h, 1, key_lanes(h), dsc) * ROOT).astype(BF16)
-    in_rest_q = [send(at_pair(far_q, i), rest_q.at[i], pair_peer[2 + i]) for i in range(2)]
-
+        normalise(h, 0, 0)
+        normalise(h, 0, 2)
     for h in range(HEADS):
         d_key, d_value = gradients(h, S2, S4)
         out123[128:384, key_lanes(h)] = d_key
@@ -412,7 +420,7 @@
         for h in range(HEADS):
             u = 2 * t + h
             if t == 0:
-                scale, center = scales[h, 0][2], centers[h, 0]
+                scale, center = scales[h, 0][3], centers[h, 0]
             else:
                 scale, center = final_in[2 * h:2 * h + 1, :], final_in[2 * h + 1:2 * h + 2, :]
             weight = scores_o[u] * scale
@@ -454,6 +462,14 @@
     acc[:, 0:LANES] += dot(spread(256, ((16, 16, 1),)), g4[0:16])
     home += [send(acc.at[128:256, :], acc_core, other)]
 
+    whole[:, cols(0)] = near_attn[0, 0:128, :]
+    grad_q[:, cols(0)] = near_q[0, 0:128, :]
+    for copy in in_near + in_rest_attn:
+        copy.wait_recv()
+    whole[:, cols(2)] = (near_attn[1, 0:128, :].astype(F32) + rest_attn[0].astype(F32)).astype(BF16)
+    whole[:, cols(3)] = (rest_attn[2].astype(F32) + rest_attn[1].astype(F32)).astype(BF16)
+    send_part[...] = dot(whole[...], w[:, far_cols]).astype(BF16)
+    part = send(send_part, recv_part, across)
     for copy in back_far:
         copy.wait_recv()
     mix = spread(128, ((2, 64, 1), (4, 32, 2), (8, 16, 4)))
@@ -468,14 +484,6 @@
         for sub in range(2)
     ]
 
-    whole[:, cols(0)] = near_attn[0, 0:128, :]
-    grad_q[:, cols(0)] = near_q[0, 0:128, :]
-    for copy in in_near + in_rest_attn:
-        copy.wait_recv()
-    whole[:, cols(2)] = (near_attn[1, 0:128, :].astype(F32) + rest_attn[0].astype(F32)).astype(BF16)
-    whole[:, cols(3)] = (rest_attn[2].astype(F32) + rest_attn[1].astype(F32)).astype(BF16)
-    send_part[...] = dot(whole[...], w[:, far_cols]).astype(BF16)
-    part = send(send_part, recv_part, across)
     for copy in in_rest_q:
         copy.wait_recv()
     grad_q[:, cols(2)] = (near_q[1, 0:128, :].astype(F32) + rest_q[0].astype(F32)).astype(BF16)
@@ -534,6 +542,7 @@
             pltpu.VMEM((4, 64, LANES), BF16),
             pltpu.VMEM((4, 32, LANES), BF16),
             pltpu.VMEM((4, 16, LANES), BF16),
+            pltpu.VMEM((32, LANES), BF16),
             pltpu.VMEM((128, LANES), BF16),
             pltpu.VMEM((64, LANES), BF16),
             pltpu.VMEM((32, LANES), BF16),

time: 51.4 us -> 50.1 us (0.975)
  Pallas kernels: 50.6 us -> 49.4 us
    pallas_call x1, Pallas kernels: 49.6 us -> 48.4 us  [local(): pl.pallas_call(kernel, out_shape=[pltpu.VMEM((B, 1024), BF16)] * 4, in_sp...]
where the time goes in v5:
time: 50.1 us; the launch traced here: 50 us
  Pallas kernels  49.4 us (99%)
  between operations  0.64 us (1%)
    pallas_call x1, Pallas kernels, local(): pl.pallas_call(kernel, out_shape=[pltpu.VMEM((B, 1024), BF16)] * 4, in_sp...  48.4 us

profile of v5, /device:TPU:1, one launch (start us, length us, event | category | flops | bytes accessed | tf_op | source)
XLA Modules:
  0.0 50.0 jit_solution(15161376632773767710)
XLA Ops:
  0.6 48.4 %shard_map.93 = (bf16[128,1024]{1,0:T(8,128)(2,1)S(1)}, bf16[128,1024]{1,0:T(8,128)(2,1)S(1)}, bf16[128,1024]{1,0:T(8,128)(2,1)S(1)}, bf16[128,1024]{1,0:T(8,128)(2,1)S(1)}) custom-call(f32[8]{0:T(128)} %slopes_in.1, bf16[128,1024]{1,0:T(8,128)(2,1)} %q.1, bf16[128,1024]{1,0:T(8,128)(2,1)} %k.1, bf16[128,1024]{1,0:T(8,128)(2,1)} %v.1, bf16[128,1024]{1,0:T(8,128)(2,1)} %g.1, ...), custom_call_target="tpu_custom_call" | custom-call | flops 2700000000 | bytes 8000000 | tf_op jit(solution)/shard_map/pallas_call | solution.py:525
  49.0 1.0 %shard_map.94 = (bf16[128,1024]{1,0:T(8,128)(2,1)}, bf16[128,1024]{1,0:T(8,128)(2,1)}, bf16[128,1024]{1,0:T(8,128)(2,1)}, bf16[128,1024]{1,0:T(8,128)(2,1)}) custom-call(bf16[128,1024]{1,0:T(8,128)(2,1)S(1)} %get-tuple-element.8.refs_0_, bf16[128,1024]{1,0:T(8,128)(2,1)S(1)} %get-tuple-element.9.refs_1_, bf16[128,1024]{1,0:T(8,128)(2,1)S(1)} %get-tuple-element.10.refs_2_, ...), custom_call_target="tpu_custom_call" | custom-call | tf_op jit(solution)/shard_map/pallas_call | solution.py:586

commit v6 on v5

--- a/solution.py
+++ b/solution.py
@@ -453,12 +453,13 @@
     g4 = dot(spread(64, ((1, 64, 1), (2, 32, 2), (4, 16, 4))), back[0]).astype(BF16)
     out[0:128, :] = (out123[0:128, :] + dot(spread(128, ((8, 16, 1),)), g4[16:32])).astype(BF16)
     out[128:256, :] = (out123[128:256, :] + dot(spread(128, ((4, 32, 1),)), g4[32:64])).astype(BF16)
-    home = [send(piece(S1 + 64 * sub, 64), zin.at[2 + sub, 0:64, :], z_peer[1][sub]) for sub in range(2)]
-    home += [
+    home = [
         send(piece(S2 + (2 * i + sub) * 32, 32), zin.at[2 * (m % 2) + sub, 64:96, :], z_peer[m][sub])
         for i, m in enumerate((2, 3))
         for sub in range(2)
     ]
+    home += [send(piece(S1 + 64 * 0, 64), zin.at[2 + 0, 0:64, :], z_peer[1][0])]
+    home += [send(piece(S1 + 64 * 1, 64), zin.at[2 + 1, 0:64, :], z_peer[1][1])]
     acc[:, 0:LANES] += dot(spread(256, ((16, 16, 1),)), g4[0:16])
     home += [send(acc.at[128:256, :], acc_core, other)]
 

time: 50.1 us -> 49.6 us (0.990)
  Pallas kernels: 49.4 us -> 48.8 us
    pallas_call x1, Pallas kernels: 48.4 us -> 47.9 us  [local(): pl.pallas_call(kernel, out_shape=[pltpu.VMEM((B, 1024), BF16)] * 4, in_sp...]
where the time goes in v6:
time: 49.6 us; the launch traced here: 49.5 us
  Pallas kernels  48.8 us (98%)
  between operations  0.64 us (1%)
    pallas_call x1, Pallas kernels, local(): pl.pallas_call(kernel, out_shape=[pltpu.VMEM((B, 1024), BF16)] * 4, in_sp...  47.9 us
    pallas_call x1, Pallas kernels, local(): pl.pallas_call(store, out_shape=[block] * 4, in_specs=[vmem] * 4, out_spe...  1 us

profile of v6, /device:TPU:1, one launch (start us, length us, event | category | flops | bytes accessed | tf_op | source)
XLA Modules:
  0.0 49.5 jit_solution(11572502449618171757)
XLA Ops:
  0.6 47.9 %shard_map.93 = (bf16[128,1024]{1,0:T(8,128)(2,1)S(1)}, bf16[128,1024]{1,0:T(8,128)(2,1)S(1)}, bf16[128,1024]{1,0:T(8,128)(2,1)S(1)}, bf16[128,1024]{1,0:T(8,128)(2,1)S(1)}) custom-call(f32[8]{0:T(128)} %slopes_in.1, bf16[128,1024]{1,0:T(8,128)(2,1)} %q.1, bf16[128,1024]{1,0:T(8,128)(2,1)} %k.1, bf16[128,1024]{1,0:T(8,128)(2,1)} %v.1, bf16[128,1024]{1,0:T(8,128)(2,1)} %g.1, ...), custom_call_target="tpu_custom_call" | custom-call | flops 2700000000 | bytes 8000000 | tf_op jit(solution)/shard_map/pallas_call | solution.py:526
  48.5 1.0 %shard_map.94 = (bf16[128,1024]{1,0:T(8,128)(2,1)}, bf16[128,1024]{1,0:T(8,128)(2,1)}, bf16[128,1024]{1,0:T(8,128)(2,1)}, bf16[128,1024]{1,0:T(8,128)(2,1)}) custom-call(bf16[128,1024]{1,0:T(8,128)(2,1)S(1)} %get-tuple-element.8.refs_0_, bf16[128,1024]{1,0:T(8,128)(2,1)S(1)} %get-tuple-element.9.refs_1_, bf16[128,1024]{1,0:T(8,128)(2,1)S(1)} %get-tuple-element.10.refs_2_, ...), custom_call_target="tpu_custom_call" | custom-call | tf_op jit(solution)/shard_map/pallas_call | solution.py:587

commit v7 on v6

--- a/solution.py
+++ b/solution.py
@@ -71,7 +71,7 @@
     layer_out, grad_q, grad_k, grad_v,
     slopes, kv, kvo, kt, qc, qm, gc, gm, gown, gfar, w, s1, s2, s3, mate3, a4, a5, a6,
     scores, gradw, prob, dsc, scores_o, gradw_o, prob_o, dsc_o, stat_out, stat_in, final_out, final_in,
-    out, out123, back, zin, acc, acc_core,
+    out, out123, back, zin, acc, acc_core, early,
     far_q, far_attn, near_q, near_attn, rest_q, rest_attn, whole, ga, send_part, recv_part,
     send_sem, recv_sem, local_sem,
 ):
@@ -494,12 +494,16 @@
     layer_out[...] = (own_part + recv_part[...].astype(F32)).astype(BF16)
 
     mix = spread(128, ((2, 64, 1), (4, 32, 1), (8, 16, 2)))
-    for copy in home:
+    for copy in home[:-8]:
         copy.wait_recv()
     bases = (acc[0:128, 0:LANES], acc_core[:, 0:LANES], acc[0:128, LANES:1024], acc_core[:, LANES:1024])
     for j, base in enumerate(bases):
         low = 64 if j < 2 else 0
-        total = (base + dot(mix[:, low:128], zin[j, low:128, :])).astype(BF16)
+        early[j] = base + dot(mix[:, low:96], zin[j, low:96, :])
+    for copy in home[-8:]:
+        copy.wait_recv()
+    for j in range(4):
+        total = (early[j] + dot(mix[:, 96:128], zin[j, 96:128, :])).astype(BF16)
         grad_k[:, cols(j)] = total[:, 0:QUARTER]
         grad_v[:, cols(j)] = total[:, QUARTER:LANES]
     for copy in started:
@@ -565,6 +569,7 @@
             pltpu.VMEM((4, 128, LANES), BF16),
             pltpu.VMEM((256, 1024), F32),
             pltpu.VMEM((128, 1024), F32),
+            pltpu.VMEM((4, 128, LANES), F32),
             pltpu.VMEM((256, QUARTER), BF16),
             pltpu.VMEM((256, QUARTER), BF16),
             pltpu.VMEM((2, 256, QUARTER), BF16),

time: 49.6 us -> 49.6 us (level)
  no operation moved by 1% of the time
where the time goes in v7:
time: 49.6 us; the launch traced here: 49.5 us
  Pallas kernels  48.9 us (99%)
  between operations  0.64 us (1%)
    pallas_call x1, Pallas kernels, local(): pl.pallas_call(kernel, out_shape=[pltpu.VMEM((B, 1024), BF16)] * 4, in_sp...  47.9 us
    pallas_call x1, Pallas kernels, local(): pl.pallas_call(store, out_shape=[block] * 4, in_specs=[vmem] * 4, out_spe...  1 us

profile of v7, /device:TPU:1, one launch (start us, length us, event | category | flops | bytes accessed | tf_op | source)
XLA Modules:
  0.0 49.5 jit_solution(11727456069220307245)
XLA Ops:
  0.6 47.9 %shard_map.93 = (bf16[128,1024]{1,0:T(8,128)(2,1)S(1)}, bf16[128,1024]{1,0:T(8,128)(2,1)S(1)}, bf16[128,1024]{1,0:T(8,128)(2,1)S(1)}, bf16[128,1024]{1,0:T(8,128)(2,1)S(1)}) custom-call(f32[8]{0:T(128)} %slopes_in.1, bf16[128,1024]{1,0:T(8,128)(2,1)} %q.1, bf16[128,1024]{1,0:T(8,128)(2,1)} %k.1, bf16[128,1024]{1,0:T(8,128)(2,1)} %v.1, bf16[128,1024]{1,0:T(8,128)(2,1)} %g.1, ...), custom_call_target="tpu_custom_call" | custom-call | flops 2700000000 | bytes 8000000 | tf_op jit(solution)/shard_map/pallas_call | solution.py:530
  48.5 1.0 %shard_map.94 = (bf16[128,1024]{1,0:T(8,128)(2,1)}, bf16[128,1024]{1,0:T(8,128)(2,1)}, bf16[128,1024]{1,0:T(8,128)(2,1)}, bf16[128,1024]{1,0:T(8,128)(2,1)}) custom-call(bf16[128,1024]{1,0:T(8,128)(2,1)S(1)} %get-tuple-element.8.refs_0_, bf16[128,1024]{1,0:T(8,128)(2,1)S(1)} %get-tuple-element.9.refs_1_, bf16[128,1024]{1,0:T(8,128)(2,1)S(1)} %get-tuple-element.10.refs_2_, ...), custom_call_target="tpu_custom_call" | custom-call | tf_op jit(solution)/shard_map/pallas_call | solution.py:592
